TPU v7x, 256 devices: a whole 4x4x8 slice. The times are simulated.
256 devices in a mesh: expert: 32 (over y, z), tensor: 8 (over x, core).
Axes of the slice: x: 4, y: 4, z: 8, core: 2. Of those that a mesh axis runs over, the one named last changes fastest.
Arguments:
- token_codes: bfloat16 [1024, 5120], P('expert', 'tensor'), may hold values from -448 to 448
- token_scale: bfloat16 [1024, 40], P('expert', 'tensor'), may hold values from 0.0019989014 to 0.019897461
- grad_out: bfloat16 [1024, 5120], P('expert', 'tensor'), may hold values from -0.59765625 to 0.59765625
- expert_ids: int32 [1024, 8], P('expert'), may hold values from 0 to 31, all different within a row; in each aligned block of 32 rows (0 to 31, 32 to 63, ...) at most 12 rows name the same one
- gate_probs: float32 [1024, 8], P('expert'), may hold values from 0.05 to 0.6
- w_in: bfloat16 [32, 2, 1536, 5120], P('expert', None, 'tensor'), may hold values from -0.078125 to 0.078125
- w_in_scale: float32 [32, 2, 1536, 40], P('expert', None, 'tensor'), may hold values from 0.5 to 2
- w_down: bfloat16 [32, 1536, 5120], P('expert', 'tensor'), may hold values from -0.15625 to 0.15625
- w_down_scale: float32 [32, 1536, 40], P('expert', 'tensor'), may hold values from 0.5 to 2
Outputs:
- grad_input: bfloat16 [1024, 5120], P('expert', 'tensor')
- grad_gates: bfloat16 [1024, 8], P('expert')
- grad_w_in: bfloat16 [32, 2, 1536, 5120], P('expert', None, 'tensor')
- grad_w_down: bfloat16 [32, 1536, 5120], P('expert', 'tensor')
Inputs may be any that keep to these rules, and one draw needn't show every extreme that they name: `expert_ids`: each row names 8 different experts. Among the 32 rows of one index of expert, no expert is named by more than 12 rows, a bound that some block reaches.
All inputs are finite; a program needn't handle non-finite values.
Results may differ from a plain program's by a relative error of at most 0.02.
Values may be sent and summed in bfloat16 or wider, within the bound.
A program may use at most 128 MiB of HBM per device.

v0:
```python
import jax
import jax.numpy as jnp
from jax import lax
from jax.sharding import PartitionSpec as P

BLOCK = 128
CAP = 12


def dequant_in(w_in, w_in_scale):
    shape_in = w_in.shape
    grouped = w_in.astype(jnp.float32).reshape(
        shape_in[0], 2, shape_in[2], shape_in[3] // BLOCK, BLOCK
    )
    return (grouped * w_in_scale[:, :, :, :, None]).astype(jnp.bfloat16).reshape(shape_in)


def dequant_down(w_down, w_down_scale):
    shape_down = w_down.shape
    grouped = w_down.astype(jnp.float32).reshape(
        shape_down[0], shape_down[1], shape_down[2] // BLOCK, BLOCK
    )
    return (grouped * w_down_scale[:, :, :, None]).astype(jnp.bfloat16).reshape(shape_down)


def on_device(
    token_codes,
    token_scale,
    grad_out,
    expert_ids,
    gate_probs,
    w_in,
    w_in_scale,
    w_down,
    w_down_scale,
):
    groups = lax.axis_size("expert")
    local_count = w_in.shape[0]
    tok_rows, per_token = expert_ids.shape
    capacity = CAP
    experts = local_count * groups
    width_local = token_codes.shape[1]
    rows_each = groups * capacity
    slot_count = tok_rows * per_token
    routed = expert_ids.reshape(-1)
    one_hot = (routed[:, None] == jnp.arange(experts, dtype=jnp.int32)[None, :]).astype(jnp.int32)
    earlier = jnp.cumsum(one_hot, axis=0) - one_hot
    position = jnp.sum(earlier * one_hot, axis=1)
    target = (routed % local_count * groups + routed // local_count) * capacity + position
    slot_source = (
        jnp.full((experts * capacity,), slot_count, jnp.int32)
        .at[target]
        .set(jnp.arange(slot_count, dtype=jnp.int32))
    )
    source = slot_source // per_token
    prob_padded = jnp.concatenate(
        [gate_probs.astype(jnp.bfloat16).reshape(-1), jnp.zeros((1,), jnp.bfloat16)], axis=0
    )
    prob_slots = jnp.take(prob_padded, slot_source, axis=0).reshape(local_count, groups, capacity)
    quantized = token_codes.reshape(tok_rows, -1, BLOCK)
    grad_blocks = grad_out.reshape(tok_rows, -1, BLOCK)
    w_in_deq = dequant_in(w_in, w_in_scale)
    w_down_deq = dequant_down(w_down, w_down_scale)

    def pack_rows(values):
        padded = jnp.concatenate([values, jnp.zeros((1,) + values.shape[1:], values.dtype)], axis=0)
        picked = jnp.take(padded, source, axis=0)
        return picked.reshape((local_count, groups, capacity) + values.shape[1:])

    def flatten_rows(values):
        return values.reshape((local_count, rows_each) + values.shape[3:])

    gathered = (
        lax.all_gather(quantized, "tensor", axis=1, tiled=True),
        lax.all_gather(token_scale, "tensor", axis=1, tiled=True),
        lax.all_gather(grad_blocks, "tensor", axis=1, tiled=True),
    )
    arrived = (
        lax.all_to_all(pack_rows(gathered[0]), "expert", split_axis=1, concat_axis=1, tiled=True),
        lax.all_to_all(pack_rows(gathered[1]), "expert", split_axis=1, concat_axis=1, tiled=True),
        lax.all_to_all(pack_rows(gathered[2]), "expert", split_axis=1, concat_axis=1, tiled=True),
        lax.all_to_all(prob_slots, "expert", split_axis=1, concat_axis=1, tiled=True),
    )
    quant_rows = flatten_rows(arrived[0])
    length = quant_rows.shape[2]
    row_values = (
        quant_rows.astype(jnp.float32) * flatten_rows(arrived[1]).astype(jnp.float32)[..., None]
    ).astype(jnp.bfloat16)
    row_values = row_values.reshape(local_count, rows_each, length * BLOCK)
    grad_values = flatten_rows(arrived[2]).reshape(local_count, rows_each, length * BLOCK)
    gate_up = jnp.einsum("erk,ejfk->ejrf", row_values, w_in_deq, preferred_element_type=jnp.float32)
    grad_hidden = jnp.einsum(
        "erk,efk->erf", grad_values, w_down_deq, preferred_element_type=jnp.float32
    )
    prob_column = arrived[3].reshape(local_count, rows_each).astype(jnp.float32)[..., None]
    gate_pre = gate_up[:, 0]
    up_pre = gate_up[:, 1]
    gate_sig = jax.nn.sigmoid(gate_pre)
    gate_act = gate_pre * gate_sig
    gate_part = jnp.sum(grad_hidden * gate_act * up_pre, axis=2)
    gate_full = grad_hidden * up_pre * gate_sig * (1.0 + gate_pre * (1.0 - gate_sig))
    up_full = grad_hidden * gate_act
    gate_grad = gate_full.astype(jnp.bfloat16)
    up_grad = up_full.astype(jnp.bfloat16)
    gate_total = lax.psum(gate_part, "tensor").astype(jnp.bfloat16)
    partial_rows = jnp.einsum(
        "erf,efd->der", gate_grad, w_in_deq[:, 0], preferred_element_type=jnp.float32
    )
    partial_rows = partial_rows + jnp.einsum(
        "erf,efd->der", up_grad, w_in_deq[:, 1], preferred_element_type=jnp.float32
    )
    slot_grad = lax.psum_scatter(
        partial_rows.reshape(
            width_local * lax.axis_size("tensor"), local_count, groups, capacity
        ).astype(jnp.bfloat16),
        "tensor",
        scatter_dimension=0,
        tiled=True,
    )
    gate_weighted = (prob_column * gate_full).astype(jnp.bfloat16)
    up_weighted = (prob_column * up_full).astype(jnp.bfloat16)
    hidden_act = (prob_column * gate_act * up_pre).astype(jnp.bfloat16)
    grad_gate_w = jnp.einsum(
        "erf,erd->efd", gate_weighted, row_values, preferred_element_type=jnp.float32
    )
    grad_up_w = jnp.einsum(
        "erf,erd->efd", up_weighted, row_values, preferred_element_type=jnp.float32
    )
    grad_w_in = jnp.stack([grad_gate_w, grad_up_w], axis=1).astype(jnp.bfloat16)
    grad_w_down = jnp.einsum(
        "erf,erd->efd", hidden_act, grad_values, preferred_element_type=jnp.float32
    ).astype(jnp.bfloat16)
    back_grad, back_gate = (
        lax.all_to_all(slot_grad, "expert", split_axis=2, concat_axis=2, tiled=True),
        lax.all_to_all(
            gate_total.reshape(1, local_count, groups, capacity),
            "expert",
            split_axis=2,
            concat_axis=2,
            tiled=True,
        ),
    )
    per_slot = jnp.take(back_grad.reshape(width_local, -1), target, axis=1).reshape(
        width_local, tok_rows, per_token
    )
    grad_input = jnp.einsum("dtk,tk->td", per_slot.astype(jnp.float32), gate_probs).astype(
        jnp.bfloat16
    )
    grad_gates = jnp.take(back_gate.reshape(-1), target).reshape(tok_rows, per_token)
    return (grad_input, grad_gates, grad_w_in, grad_w_down)


def solution(mesh):
    placed = (
        P("expert", "tensor"),
        P("expert", "tensor"),
        P("expert", "tensor"),
        P("expert", None),
        P("expert", None),
        P("expert", None, "tensor", None),
        P("expert", None, "tensor", None),
        P("expert", "tensor", None),
        P("expert", "tensor", None),
    )
    return jax.shard_map(
        on_device,
        mesh=mesh,
        in_specs=placed,
        out_specs=(
            P("expert", "tensor"),
            P("expert", None),
            P("expert", None, "tensor", None),
            P("expert", "tensor", None),
        ),
        check_vma=False,
    )
```

profile of v0, /device:TPU:8, one launch (start us, length us, event | category | flops | bytes accessed | tf_op | source)
XLA Modules:
  0.0 417.5 jit_solution(13336362370326277954)
XLA Ops:
  8.1 12.1 %all-gather = bf16[8,5,32]{2,1,0:T(8,128)(2,1)S(1)} all-gather(bf16[1,5,32]{2,1,0:T(8,128)(2,1)} %bitcast.188), channel_id=1, replica_groups=mesh['expert'=32,'tensor'=8] {'tensor'}, dimensions={0}, use_global_device_ids=true | all-gather | bytes 2880 | tf_op jit(solution)/shard_map/all_gather | solution.py:75
  25.4 11.7 %all-to-all-start.2 = ((bf16[32,2,240]{2,1,0:T(2,128)(2,1)}), bf16[32,2,240]{2,1,0:T(2,128)(2,1)S(1)}, u32[]{:S(2)}, u32[]{:S(2)}) async-start(bf16[32,2,240]{2,1,0:T(2,128)(2,1)} %reshape.485), calls=%async_computation.2 | async-start | bytes 65536 | tf_op jit(solution)/shard_map/all_to_all | solution.py:80
  37.1 12.9 %all_gather.10 = bf16[32,40,128]{2,0,1:T(8,128)(2,1)S(1)} all-gather(bf16[32,5,128]{2,0,1:T(8,128)(2,1)S(1)} %copy_bitcast_fusion), channel_id=1, replica_groups=mesh['expert'=32,'tensor'=8] {'tensor'}, dimensions={1}, use_global_device_ids=true | all-gather | bytes 368640 | tf_op jit(solution)/shard_map/all_gather | solution.py:74
  50.2 3.5 gather_fusion.5
  53.7 12.9 %all_gather.9 = bf16[32,40,128]{2,0,1:T(8,128)(2,1)S(1)} all-gather(bf16[32,5,128]{2,0,1:T(8,128)(2,1)S(1)} %copy_bitcast_fusion.1), channel_id=1, replica_groups=mesh['expert'=32,'tensor'=8] {'tensor'}, dimensions={1}, use_global_device_ids=true | all-gather | bytes 368640 | tf_op jit(solution)/shard_map/all_gather | solution.py:76
  66.8 3.6 gather_fusion.4
  70.4 6.1 %broadcast_select_fusion = (bf16[384,40,128]{2,1,0:T(8,128)(2,1)}, bf16[384,40,128]{2,1,0:T(8,128)(2,1)}) fusion(bf16[384,40,128]{2,1,0:T(8,128)(2,1)} %gather_fusion.5, pred[384]{0:T(512)(128)(4,1)S(1)} %get-tuple-element.19, bf16[384,40,128]{2,1,0:T(8,128)(2,1)} %gather_fusion.4), kind=kLoop, calls=%fused_computation.26 | loop fusion | flops 3932160 | bytes 15729024 | tf_op jit(solution)/shard_map/jit(_take)/select_n | solution.py:67
  76.5 98.4 %all_to_all.30 = bf16[1,32,12,40,128]{4,3,2,0,1:T(8,128)(2,1)} all-to-all(bf16[1,32,12,40,128]{4,3,2,0,1:T(8,128)(2,1)} %bitcast.177), channel_id=1, replica_groups=mesh['expert'=32,'tensor'=8] {'expert'}, dimensions={1} | all-to-all | bytes 7864320 | tf_op jit(solution)/shard_map/all_to_all | solution.py:79
  174.9 7.7 %all-to-all-start = ((bf16[1,32,12,40,128]{4,3,2,0,1:T(8,128)(2,1)}), bf16[1,32,12,40,128]{4,3,2,0,1:T(8,128)(2,1)}, u32[]{:S(2)}, u32[]{:S(2)}) async-start(bf16[1,32,12,40,128]{4,3,2,0,1:T(8,128)(2,1)} %bitcast.176), calls=%async_computation | async-start | bytes 7864320 | tf_op jit(solution)/shard_map/all_to_all | solution.py:81
  183.0 5.2 %mul.162 = f32[2,192,40,128]{3,2,1,0:T(8,128)} broadcast(f32[2,192,40]{2,1,0:T(8,128)S(1)} %copy.47), dimensions={0,1,2} | broadcast | bytes 7925760 | tf_op jit(solution)/shard_map/mul | solution.py:15
  188.1 9.2 %mul.163 = f32[1,2,192,5120]{3,2,1,0:T(8,128)} reshape(f32[2,192,40,128]{3,2,1,0:T(8,128)} %mul.162) | data formatting | bytes 15728640 | tf_op jit(solution)/shard_map/mul | solution.py:15
  199.9 4.9 %mul.168 = f32[1,192,5120]{2,1,0:T(8,128)} reshape(f32[192,40,128]{2,1,0:T(8,128)} %mul.167) | data formatting | bytes 7864320 | tf_op jit(solution)/shard_map/mul | solution.py:23
  204.8 7.5 %multiply_convert_fusion = bf16[1,2,192,5120]{3,2,1,0:T(8,128)(2,1)} fusion(f32[1,2,192,5120]{3,2,1,0:T(8,128)} %mul.163, bf16[1,2,192,5120]{3,2,1,0:T(8,128)(2,1)} %param.16), kind=kLoop, calls=%fused_computation.12 | loop fusion | flops 5898240 | bytes 15728640 | tf_op jit(solution)/shard_map/convert_element_type | solution.py:15
  212.5 5.6 %fusion.1 = bf16[384,40,128]{2,1,0:T(8,128)(2,1)} fusion(f32[384,40]{1,0:T(8,128)S(1)} %reshape.395, bf16[1,32,12,40,128]{4,3,2,0,1:T(8,128)(2,1)} %all_to_all.30), kind=kLoop, calls=%fused_computation.10 | loop fusion | flops 5898240 | bytes 7925760 | tf_op jit(solution)/shard_map/convert_element_type | solution.py:88
  218.1 6.9 %reshape.464 = bf16[384,5120,1]{1,0,2:T(8,128)(2,1)} reshape(bf16[384,40,128]{2,1,0:T(8,128)(2,1)} %fusion.1) | data formatting | bytes 7864320 | tf_op jit(solution)/shard_map/convert_element_type | solution.py:88
  225.1 5.6 %fusion.15 = f32[1,2,384,192]{2,3,1,0:T(8,128)S(1)} fusion(bf16[384,5120,1]{1,0,2:T(8,128)(2,1)} %reshape.464, bf16[1,2,192,5120]{3,2,1,0:T(8,128)(2,1)} %multiply_convert_fusion), kind=kOutput, calls=%fused_computation.34 | convolution fusion | flops 1509949440 | bytes 8454144 | tf_op jit(solution)/shard_map/erk,ejfk->ejrf/dot_general | solution.py:91
  230.7 39.9 %all-to-all-done = bf16[1,32,12,40,128]{4,3,2,0,1:T(8,128)(2,1)} async-done(((bf16[1,32,12,40,128]{4,3,2,0,1:T(8,128)(2,1)}), bf16[1,32,12,40,128]{4,3,2,0,1:T(8,128)(2,1)}, u32[]{:S(2)}, u32[]{:S(2)}) %all-to-all-start) | async-done | bytes 3932192 | tf_op jit(solution)/shard_map/all_to_all | solution.py:81
  270.6 5.0 %fusion.27 = (f32[384]{0:T(512)S(1)}, f32[384,192]{0,1:T(8,128)S(1)}) fusion(f32[1,2,384,192]{2,3,1,0:T(8,128)S(1)} %fusion.15, f32[1,192,5120]{2,1,0:T(8,128)} %mul.168, bf16[1,192,5120]{2,1,0:T(8,128)(2,1)S(1)} %copy-done.14, bf16[48,8,40,128]{3,2,1,0:T(8,128)(2,1)} %bitcast.46), kind=kOutput, calls=%fused_computation.50 | convolution fusion | flops 758439552 | bytes 10716672 | tf_op jit(solution)/shard_map/erk,efk->erf/dot_general | solution.py:92
  280.1 6.3 %copy.66 = bf16[5120,384]{1,0:T(8,128)(2,1)} copy(bf16[5120,384]{0,1:T(8,128)(2,1)} %add_convert_fusion) | data formatting | bytes 7864320
  290.8 7.8 %all-to-all-start.5 = ((bf16[1,32,12]{2,0,1:T(2,128)(2,1)}), bf16[1,32,12]{2,0,1:T(2,128)(2,1)S(1)}, u32[]{:S(2)}, u32[]{:S(2)}) async-start(bf16[1,32,12]{2,0,1:T(2,128)(2,1)} %select_n.109), calls=%async_computation.5 | async-start | bytes 32768 | tf_op jit(solution)/shard_map/all_to_all | solution.py:82
  300.1 7.1 %all-to-all-done.5 = bf16[1,32,12]{2,0,1:T(2,128)(2,1)S(1)} async-done(((bf16[1,32,12]{2,0,1:T(2,128)(2,1)}), bf16[1,32,12]{2,0,1:T(2,128)(2,1)S(1)}, u32[]{:S(2)}, u32[]{:S(2)}) %all-to-all-start.5) | async-done | bytes 800 | tf_op jit(solution)/shard_map/all_to_all | solution.py:82
  307.4 23.6 %psum.7 = bf16[1,384]{1,0:T(2,128)(2,1)S(1)} all-reduce(f32[1,384]{1,0:T(1,128)S(1)} %reduce_sum.28), channel_id=1, replica_groups=mesh['expert'=32,'tensor'=8] {'tensor'}, use_global_device_ids=true, to_apply=%region_6.8 | all-reduce | flops 384 | bytes 2304 | tf_op jit(solution)/shard_map/psum | solution.py:105
  331.7 4.9 %all-to-all-start.4 = ((bf16[1,1,32,12]{3,1,0,2:T(2,128)(2,1)}), bf16[1,1,32,12]{3,1,0,2:T(2,128)(2,1)S(1)}, u32[]{:S(2)}, u32[]{:S(2)}) async-start(bf16[1,1,32,12]{3,1,0,2:T(2,128)(2,1)} %reshape.468), calls=%async_computation.4 | async-start | bytes 32768 | tf_op jit(solution)/shard_map/all_to_all | solution.py:135
  336.7 6.2 %convert.26 = f32[48,8,40,128]{3,2,1,0:T(8,128)} convert(bf16[48,8,40,128]{3,2,1,0:T(8,128)(2,1)} %bitcast.174) | non-fusion elementwise | flops 1966080 | bytes 11796480
  342.9 4.6 %fusion.4 = bf16[1,192,5120]{2,1,0:T(8,128)(2,1)} fusion(bf16[48,8,40,128]{3,2,1,0:T(8,128)(2,1)} %bitcast.46, f32[1,2,384,192]{2,3,1,0:T(8,128)S(1)} %fusion.15, f32[384]{0:T(512)S(1)} %reshape.396), kind=kOutput, calls=%fused_computation.18 | convolution fusion | flops 756473856 | bytes 6489600 | tf_op jit(solution)/shard_map/erf,erd->efd/dot_general | solution.py:130
  347.5 5.1 %mul.170 = f32[384,40,128]{2,1,0:T(8,128)} broadcast(f32[384,40]{1,0:T(8,128)S(1)} %reshape.395), dimensions={0,1} | broadcast | bytes 7925760 | tf_op jit(solution)/shard_map/mul | solution.py:87
  352.6 7.6 %fusion = bf16[384,5120]{1,0:T(8,128)(2,1)S(1)} fusion(f32[48,8,40,128]{3,2,1,0:T(8,128)} %bitcast.175, f32[48,8,40,128]{3,2,1,0:T(8,128)} %convert.26), kind=kLoop, calls=%fused_computation.8 | loop fusion | flops 3932160 | bytes 19660800 | tf_op jit(solution)/shard_map/convert_element_type | solution.py:88
  363.5 13.9 %reshape.470 = bf16[640,1,32,12]{3,2,1,0:T(8,128)(2,1)} reshape(bf16[640,384]{1,0:T(8,128)(2,1)} %reduce-scatter.4.cloned.1.call-done) | data formatting | bytes 983040
  377.3 6.3 %copy.65 = bf16[640,1,32,12]{0,3,2,1:T(8,128)(2,1)} copy(bf16[640,1,32,12]{3,2,1,0:T(8,128)(2,1)} %reshape.470) | data formatting | bytes 983040
  383.6 9.8 %all-to-all-start.3 = ((bf16[640,1,32,12]{0,3,1,2:T(8,128)(2,1)}), bf16[640,1,32,12]{0,3,1,2:T(8,128)(2,1)S(1)}, u32[]{:S(2)}, u32[]{:S(2)}) async-start(bf16[640,1,32,12]{0,3,1,2:T(8,128)(2,1)} %bitcast.178), calls=%async_computation.3 | async-start | bytes 1310720 | tf_op jit(solution)/shard_map/all_to_all | solution.py:134
  393.5 3.3 fusion.3
  402.0 6.4 %all-to-all-done.3 = bf16[640,1,32,12]{0,3,1,2:T(8,128)(2,1)S(1)} async-done(((bf16[640,1,32,12]{0,3,1,2:T(8,128)(2,1)}), bf16[640,1,32,12]{0,3,1,2:T(8,128)(2,1)S(1)}, u32[]{:S(2)}, u32[]{:S(2)}) %all-to-all-start.3) | async-done | bytes 491552 | tf_op jit(solution)/shard_map/all_to_all | solution.py:134
  (101 shorter events, 31.3 us)
Async XLA Ops:
  7.2 29.9 %copy-start = (bf16[32,640]{1,0:T(8,128)(2,1)S(1)}, bf16[32,640]{1,0:T(8,128)(2,1)}, u32[]{:S(2)}) copy-start(bf16[32,640]{1,0:T(8,128)(2,1)} %param.11) | copy-start | bytes 122884
  8.0 14.9 %copy-start.4 = (s32[32,8]{1,0:T(8,128)}, s32[32,8]{1,0:T(8,128)S(1)}, u32[]{:S(2)}) copy-start(s32[32,8]{1,0:T(8,128)S(1)} %copy.43) | copy-start | bytes 3076
  25.4 51.2 %all-to-all-start.2 = ((bf16[32,2,240]{2,1,0:T(2,128)(2,1)}), bf16[32,2,240]{2,1,0:T(2,128)(2,1)S(1)}, u32[]{:S(2)}, u32[]{:S(2)}) async-start(bf16[32,2,240]{2,1,0:T(2,128)(2,1)} %reshape.485), calls=%async_computation.2 | async-start | bytes 65536 | tf_op jit(solution)/shard_map/all_to_all | solution.py:80
  50.2 3.6 copy-start.10
  174.9 7.9 %copy-start.6 = (f32[1,2,192,40]{2,3,1,0:T(8,128)S(1)}, f32[1,2,192,40]{2,3,1,0:T(8,128)}, u32[]{:S(2)}) copy-start(f32[1,2,192,40]{2,3,1,0:T(8,128)} %param.17) | copy-start | bytes 184324
  174.9 95.7 %all-to-all-start = ((bf16[1,32,12,40,128]{4,3,2,0,1:T(8,128)(2,1)}), bf16[1,32,12,40,128]{4,3,2,0,1:T(8,128)(2,1)}, u32[]{:S(2)}, u32[]{:S(2)}) async-start(bf16[1,32,12,40,128]{4,3,2,0,1:T(8,128)(2,1)} %bitcast.176), calls=%async_computation | async-start | bytes 7864320 | tf_op jit(solution)/shard_map/all_to_all | solution.py:81
  182.6 180.9 %reduce-scatter.4.cloned.1.call-start = ((), (), s32[]{:S(2)}) async-start(), calls=%async_computation.7 | async-start | bytes 4423680
  188.1 9.2 %copy-start.11 = (f32[1,192,40]{1,2,0:T(8,128)S(1)}, f32[1,192,40]{1,2,0:T(8,128)}, u32[]{:S(2)}) copy-start(f32[1,192,40]{1,2,0:T(8,128)} %param.19) | copy-start | bytes 92164
  225.0 45.6 %copy-start.14 = (bf16[1,192,5120]{2,1,0:T(8,128)(2,1)S(1)}, bf16[1,192,5120]{2,1,0:T(8,128)(2,1)}, u32[]{:S(2)}) copy-start(bf16[1,192,5120]{2,1,0:T(8,128)(2,1)} %param.18) | copy-start | bytes 5898244
  270.6 5.0 %copy-start.3 = (bf16[1,2,192,5120]{3,2,1,0:T(8,128)(2,1)S(1)}, bf16[1,2,192,5120]{3,2,1,0:T(8,128)(2,1)}, u32[]{:S(2)}) copy-start(bf16[1,2,192,5120]{3,2,1,0:T(8,128)(2,1)} %multiply_convert_fusion) | copy-start | bytes 11796484
  286.3 0.7 copy-start.13
  290.8 16.4 %all-to-all-start.5 = ((bf16[1,32,12]{2,0,1:T(2,128)(2,1)}), bf16[1,32,12]{2,0,1:T(2,128)(2,1)S(1)}, u32[]{:S(2)}, u32[]{:S(2)}) async-start(bf16[1,32,12]{2,0,1:T(2,128)(2,1)} %select_n.109), calls=%async_computation.5 | async-start | bytes 32768 | tf_op jit(solution)/shard_map/all_to_all | solution.py:82
  331.7 51.9 %all-to-all-start.4 = ((bf16[1,1,32,12]{3,1,0,2:T(2,128)(2,1)}), bf16[1,1,32,12]{3,1,0,2:T(2,128)(2,1)S(1)}, u32[]{:S(2)}, u32[]{:S(2)}) async-start(bf16[1,1,32,12]{3,1,0,2:T(2,128)(2,1)} %reshape.468), calls=%async_computation.4 | async-start | bytes 32768 | tf_op jit(solution)/shard_map/all_to_all | solution.py:135
  360.3 1.9 copy-start.2
  383.6 9.9 %copy-start.8 = (bf16[1,1,32,12]{3,1,0,2:T(2,128)(2,1)}, bf16[1,1,32,12]{3,1,0,2:T(2,128)(2,1)S(1)}, u32[]{:S(2)}) copy-start(bf16[1,1,32,12]{3,1,0,2:T(2,128)(2,1)S(1)} %all-to-all-done.4) | copy-start | bytes 2308
  383.6 24.8 %all-to-all-start.3 = ((bf16[640,1,32,12]{0,3,1,2:T(8,128)(2,1)}), bf16[640,1,32,12]{0,3,1,2:T(8,128)(2,1)S(1)}, u32[]{:S(2)}, u32[]{:S(2)}) async-start(bf16[640,1,32,12]{0,3,1,2:T(8,128)(2,1)} %bitcast.178), calls=%async_computation.3 | async-start | bytes 1310720 | tf_op jit(solution)/shard_map/all_to_all | solution.py:134
  396.8 2.3 copy-start.9
  396.8 4.5 %copy-start.5 = (s32[32,8]{1,0:T(8,128)S(1)}, s32[32,8]{1,0:T(8,128)}, u32[]{:S(2)}) copy-start(s32[32,8]{1,0:T(8,128)} %copy-done.4) | copy-start | bytes 3076
  396.8 4.5 %copy-start.7 = (s32[32,8]{1,0:T(8,128)S(1)}, s32[32,8]{1,0:T(8,128)}, u32[]{:S(2)}) copy-start(s32[32,8]{1,0:T(8,128)} %reduce_sum.25) | copy-start | bytes 3076
  396.8 13.9 %copy-start.1 = (bf16[32,640]{1,0:T(8,128)(2,1)S(1)}, bf16[32,640]{1,0:T(8,128)(2,1)}, u32[]{:S(2)}) copy-start(bf16[32,640]{1,0:T(8,128)(2,1)} %param.11) | copy-start | bytes 122884
  399.1 10.6 %copy-start.12 = (bf16[32,8,1]{1,2,0:T(2,128)(2,1)S(1)}, bf16[32,8,1]{1,2,0:T(2,128)(2,1)}, u32[]{:S(2)}) copy-start(bf16[32,8,1]{1,2,0:T(2,128)(2,1)} %copy.62) | copy-start | bytes 1540
Sparse Core Ops, SparseCore 0:
  286.5 37.9 reduce-scatter.3
where the time goes:
time: 421 us; the launch traced here: 418 us
  blocking collectives  160 us (38%)
  local copies, waits for them, and re-layouts  86.5 us (21%)
  waiting for transfers between devices  53.5 us (13%)
  starting transfers between devices  42.2 us (10%)
  other arithmetic  36.4 us (9%)
  matrix products  24.6 us (6%)
  between operations  14.5 us (3%)
    all_to_all x1, blocking collectives, on_device(): lax.all_to_all(pack_rows(gathered[0]), 'expert', split_axis=1, concat_axi...  98.4 us
    all_to_all x1, waiting for transfers between devices, on_device(): lax.all_to_all(pack_rows(gathered[2]), 'expert', split_axis=1, concat_axi...  39.9 us
    unnamed x40, local copies, waits for them, and re-layouts  32.2 us
    psum x1, blocking collectives, on_device(): gate_total = lax.psum(gate_part, 'tensor').astype(jnp.bfloat16)  23.6 us
    mul x3, local copies, waits for them, and re-layouts, dequant_in(): grouped * w_in_scale[:, :, :, :, None]  14.4 us
    convert_element_type x2, other arithmetic, on_device(): row_values = (quant_rows.astype(jnp.float32) * flatten_rows(arrived[1]).a...  13.3 us
    all_gather x1, blocking collectives, on_device(): lax.all_gather(grad_blocks, 'tensor', axis=1, tiled=True)  12.9 us
    all_gather x1, blocking collectives, on_device(): lax.all_gather(quantized, 'tensor', axis=1, tiled=True)  12.9 us
  transfers between devices with their start and end apart: 6, of which 3 were waited for; matrix products, arithmetic and copies ran while one was open for 29% of the time, Pallas kernels for 0%

commit v1 on v0

v1 whole, which is shorter than its diff:
```python
import functools

import jax
import jax.numpy as jnp
from jax import lax
from jax.experimental import pallas as pl
from jax.experimental.pallas import tpu as pltpu
from jax.sharding import PartitionSpec as P

MESH = pl.DeviceIdType.MESH
BLOCK = 128
CAP = 12
PAD = 16
NX, NY, NZ = 4, 4, 8
NE = NY * NZ
TOK = 32
TOP = 8
WL = 640
WIDTH = 5120
HID = 192
ROWS = NE * CAP
CH = NZ * CAP
CHP = NZ * PAD
RS = CH + 16
HALF = CH // 2
F32 = jnp.float32
BF16 = jnp.bfloat16


def mm(a, b, dims):
    return lax.dot_general(a, b, (dims, ((), ())), preferred_element_type=F32)


def iota(shape, axis):
    return lax.broadcasted_iota(jnp.int32, shape, axis)


def onehot(mask):
    return jnp.where(mask, 1.0, 0.0).astype(BF16)


def exchange(
    ids_t, prob_t, ids, codes, tok_scale, grad_out, in_scale, down_scale, w_in, w_down,
    gi_out, gg_out, hid_out, rows_out,
    send, recv, own, rows, weights, parts, core_in, far_sum, plus_sum, minus_sum,
    relay_a, relay_b, from_minus, from_plus, back_send, back_recv, chosen, prob_col,
    sem_w, sem_own, sem_out, a_s, a_r, g_s, g_r, r_s, r_r, b_s, b_r,
):
    er = lax.axis_index("expert")
    te = lax.axis_index("tensor")
    y, z = lax.div(er, NZ), lax.rem(er, NZ)
    x, core = lax.div(te, 2), lax.rem(te, 2)
    other = 1 - core
    x_plus, x_minus, x_far = lax.rem(x + 1, NX), lax.rem(x + 3, NX), lax.rem(x + 2, NX)
    t_plus, t_minus, t_far = x_plus * 2 + core, x_minus * 2 + core, x_far * 2 + core
    t_core = x * 2 + other

    def ahead(rel):
        dy, dz = lax.div(rel, NZ), lax.rem(rel, NZ)
        return lax.rem(y + dy, NY) * NZ + lax.rem(z + dz, NZ)

    def behind(rel):
        dy, dz = lax.div(rel, NZ), lax.rem(rel, NZ)
        return lax.rem(y + NY - dy, NY) * NZ + lax.rem(z + NZ - dz, NZ)

    barrier = pltpu.get_barrier_semaphore()

    @pl.loop(1, NE)
    def _(rel):
        pl.semaphore_signal(barrier, inc=1, device_id=(ahead(rel), te), device_id_type=MESH)

    for peer in (t_plus, t_minus, t_core):
        pl.semaphore_signal(barrier, inc=1, device_id=(er, peer), device_id_type=MESH)

    load_in = pltpu.make_async_copy(w_in, weights.at[pl.ds(0, 2 * HID), :], sem_w.at[0])
    load_down = pltpu.make_async_copy(w_down, weights.at[pl.ds(2 * HID, HID), :], sem_w.at[1])
    load_in.start()
    load_down.start()

    slot = iota((NE * PAD, 128), 0)
    rel_of = slot >> 4
    r_of = slot & 15
    expert_of = ((y + (rel_of >> 3)) & 3) * NZ + ((z + (rel_of & 7)) & 7)
    weight = jnp.zeros((NE * PAD, 128), F32)
    for k in range(TOP):
        weight = weight + jnp.where(ids_t[k : k + 1, :] == expert_of, prob_t[k : k + 1, :], 0.0)
    before = onehot(iota((128, 128), 0) < iota((128, 128), 1))
    place = mm(onehot(weight > 0.0), before, ((1,), (0,)))
    mine = jnp.logical_and(weight > 0.0, place == r_of.astype(F32))
    pick = onehot(mine)[:, :TOK]
    kept = jnp.where(mine, weight, 0.0)
    kept_high = kept.astype(BF16)
    chosen[0] = kept_high
    chosen[1] = (kept - kept_high.astype(F32)).astype(BF16)
    for j in range(WL // BLOCK):
        cols = slice(j * BLOCK, (j + 1) * BLOCK)
        values = (codes[:, cols].astype(F32) * tok_scale[:, j : j + 1].astype(F32)).astype(BF16)
        packed = mm(pick, values, ((1,), (0,)))
        if j == 0:
            packed = packed + jnp.where(r_of == CAP, weight, 0.0)
        send[:, cols] = packed.astype(BF16)
    send[:, WL:] = mm(pick, grad_out[...], ((1,), (0,))).astype(BF16)
    recv[0:PAD, :] = send[0:PAD, :]

    pl.semaphore_wait(barrier, NE - 1 + 3)

    def at16(ref, rel):
        return ref.at[pl.ds(pl.multiple_of(rel * PAD, PAD), PAD), :]

    def out_copy(rel):
        return pltpu.make_async_remote_copy(
            src_ref=at16(send, rel), dst_ref=at16(recv, rel), send_sem=a_s.at[rel], recv_sem=a_r.at[rel],
            device_id=(ahead(rel), te), device_id_type=MESH,
        )

    def back_copy(rel):
        return pltpu.make_async_remote_copy(
            src_ref=at16(back_send, rel), dst_ref=at16(back_recv, rel), send_sem=b_s.at[rel], recv_sem=b_r.at[rel],
            device_id=(behind(rel), te), device_id_type=MESH,
        )

    @pl.loop(1, NE)
    def _(rel):
        out_copy(rel).start()

    def cols_of(t):
        return pl.ds(pl.multiple_of(t * WL, BLOCK), WL)

    def window(c, t, first=0, count=CH):
        return rows.at[:, pl.ds(pl.multiple_of(c * CH + first, 16), count), cols_of(t)]

    def own_rows(c):
        return own.at[:, pl.ds(pl.multiple_of(c * CH, 16), CH), :]

    def own_copy(c):
        return pltpu.make_async_copy(own_rows(c), window(c, te), sem_own.at[c])

    def gather_copy(c, k):
        ref, peer = (
            (lambda: window(c, te), t_plus),
            (lambda: window(c, te), t_minus),
            (lambda: window(c, te), t_core),
            (lambda: window(c, t_minus, 0, HALF), t_plus),
            (lambda: window(c, t_plus, HALF, HALF), t_minus),
            (lambda: window(c, t_minus), t_core),
            (lambda: window(c, t_plus), t_core),
            (lambda: window(c, t_far), t_core),
        )[k]
        ref = ref()
        return pltpu.make_async_remote_copy(
            src_ref=own_rows(c) if k < 3 else ref, dst_ref=ref, send_sem=g_s.at[k, c], recv_sem=g_r.at[k, c],
            device_id=(er, peer), device_id_type=MESH,
        )

    to_core = (x_far * 2 + other, x_plus * 2 + other, x_minus * 2 + other, t_core)

    def sum_copy(c, k):
        if k < 4:
            src, dst, peer = parts.at[c, :, cols_of(to_core[k])], core_in.at[k, c], t_core
        elif k == 4:
            src, dst, peer = far_sum.at[c, pl.ds(0, HALF), :], relay_a.at[c], t_plus
        elif k == 5:
            src, dst, peer = far_sum.at[c, pl.ds(HALF, RS - HALF), :], relay_b.at[c], t_minus
        elif k == 6:
            src, dst, peer = plus_sum.at[c], from_minus.at[c], t_plus
        else:
            src, dst, peer = minus_sum.at[c], from_plus.at[c], t_minus
        return pltpu.make_async_remote_copy(
            src_ref=src, dst_ref=dst, send_sem=r_s.at[k, c], recv_sem=r_r.at[k, c],
            device_id=(er, peer), device_id_type=MESH,
        )

    def rows_copy(c):
        span = pl.ds(pl.multiple_of(c * CH, 16), CH)
        return pltpu.make_async_copy(rows.at[:, span, :], rows_out.at[:, span, :], sem_out.at[c])

    load_in.wait()
    load_down.wait()

    def scale_rows(scale_ref, first, count):
        @pl.loop(0, count // 16)
        def _(i):
            at = pl.ds(pl.multiple_of(i * 16, 16), 16)
            to = pl.ds(pl.multiple_of(first + i * 16, 16), 16)
            scale = scale_ref[at, :]
            for q in range(WIDTH // BLOCK):
                cols = slice(q * BLOCK, (q + 1) * BLOCK)
                weights[to, cols] = (weights[to, cols].astype(F32) * scale[:, q : q + 1]).astype(BF16)

    scale_rows(in_scale, 0, 2 * HID)
    scale_rows(down_scale, 2 * HID, HID)

    def dispatch_stage(c):
        @pl.loop(0, NZ)
        def _(i):
            rel = c * NZ + i

            @pl.when(rel > 0)
            def _():
                out_copy(rel).wait_recv()

        row = iota((CH, CHP), 0)
        col = iota((CH, CHP), 1)
        group = lax.div(row, CAP)
        within = row - group * CAP
        squeeze = onehot(col == group * PAD + within)
        span = pl.ds(pl.multiple_of(c * CH, 16), CH)
        part = pl.ds(pl.multiple_of(c * CHP, CHP), CHP)
        own[0, span, :] = mm(squeeze, recv[part, :WL], ((1,), (0,))).astype(BF16)
        own[1, span, :] = mm(squeeze, recv[part, WL:], ((1,), (0,))).astype(BF16)
        own_copy(c).start()
        for k in (0, 1, 2):
            gather_copy(c, k).start()
        named = mm(onehot(col == group * PAD + CAP), recv[part, :BLOCK], ((1,), (0,)))
        rank = mm(onehot(named > 0.0), before, ((1,), (0,)))
        taken = jnp.logical_and(named > 0.0, rank == within.astype(F32))
        prob_col[span, :] = jnp.sum(jnp.where(taken, named, 0.0), axis=1, keepdims=True)

    def relay_stage(c):
        gather_copy(c, 0).wait_recv()
        gather_copy(c, 3).start()
        gather_copy(c, 5).start()
        gather_copy(c, 1).wait_recv()
        gather_copy(c, 4).start()
        gather_copy(c, 6).start()

    def far_stage(c):
        gather_copy(c, 3).wait_recv()
        gather_copy(c, 4).wait_recv()
        gather_copy(c, 7).start()

    def compute_stage(c):
        for k in (2, 5, 6, 7):
            gather_copy(c, k).wait_recv()
        own_copy(c).wait()
        rows_copy(c).start()
        span = pl.ds(pl.multiple_of(c * CH, 16), CH)
        row_values = rows[0, span, :]
        gate = mm(row_values, weights[0:HID, :], ((1,), (1,)))
        up = mm(row_values, weights[HID : 2 * HID, :], ((1,), (1,)))
        hidden = mm(rows[1, span, :], weights[2 * HID :, :], ((1,), (1,)))
        sig = jax.nn.sigmoid(gate)
        act = gate * sig
        gate_full = hidden * up * sig * (1.0 + gate * (1.0 - sig))
        up_full = hidden * act
        gate_grad = gate_full.astype(BF16)
        up_grad = up_full.astype(BF16)
        acted = act * up
        share = hidden * acted
        share_high = share.astype(BF16)
        ones = jnp.ones((16, HID), BF16)
        gate_row = mm(ones, share_high, ((1,), (1,))) + mm(
            ones, (share - share_high.astype(F32)).astype(BF16), ((1,), (1,))
        )
        gate_row = gate_row.astype(BF16)
        for t in range(2 * NX):
            cols = slice(t * WL, (t + 1) * WL)
            part = mm(gate_grad, weights[0:HID, cols], ((1,), (0,)))
            part = part + mm(up_grad, weights[HID : 2 * HID, cols], ((1,), (0,)))
            parts[c, 0:CH, cols] = part.astype(BF16)
            parts[c, CH:RS, cols] = jnp.zeros((16, WL), BF16)
            parts[c, CH:RS, t * WL : t * WL + CH] = gate_row
        for k in range(4):
            sum_copy(c, k).start()
        prob = prob_col[span, :]
        hid_out[0, span, :] = (prob * gate_full).astype(BF16)
        hid_out[1, span, :] = (prob * up_full).astype(BF16)
        hid_out[2, span, :] = (prob * acted).astype(BF16)

    def chip_sum(c, k, t):
        return parts[c, :, cols_of(t)].astype(F32) + core_in[k, c].astype(F32)

    def core_stage(c):
        sum_copy(c, 0).wait_recv()
        far_sum[c] = chip_sum(c, 0, t_far).astype(BF16)
        sum_copy(c, 4).start()
        sum_copy(c, 5).start()

    def ring_stage(c):
        sum_copy(c, 1).wait_recv()
        total = chip_sum(c, 1, t_plus)
        sum_copy(c, 4).wait_recv()
        plus_sum[c, 0:HALF, :] = (total[0:HALF] + relay_a[c].astype(F32)).astype(BF16)
        plus_sum[c, HALF:RS, :] = total[HALF:RS].astype(BF16)
        sum_copy(c, 6).start()
        sum_copy(c, 2).wait_recv()
        total = chip_sum(c, 2, t_minus)
        sum_copy(c, 5).wait_recv()
        minus_sum[c, 0:HALF, :] = total[0:HALF].astype(BF16)
        minus_sum[c, HALF:RS, :] = (total[HALF:RS] + relay_b[c].astype(F32)).astype(BF16)
        sum_copy(c, 7).start()

    def return_stage(c):
        sum_copy(c, 3).wait_recv()
        total = chip_sum(c, 3, te)
        sum_copy(c, 6).wait_recv()
        sum_copy(c, 7).wait_recv()
        total = total + from_minus[c].astype(F32) + from_plus[c].astype(F32)
        row = iota((CHP, CH), 0)
        col = iota((CHP, CH), 1)
        spread = onehot(jnp.logical_and((row & 15) < CAP, col == (row >> 4) * CAP + (row & 15)))
        out = mm(spread, total[0:CH].astype(BF16), ((1,), (0,)))
        r = iota((CHP, WL), 0) & 15
        out = out + jnp.where(r == CAP, total[CH : CH + 1, :], 0.0)
        at = pl.ds(pl.multiple_of(c * CHP, CHP), CHP)
        back_send[at, :] = out.astype(BF16)

        @pl.loop(0, NZ)
        def _(i):
            rel = c * NZ + i

            @pl.when(rel > 0)
            def _():
                back_copy(rel).start()

    stages = (
        (dispatch_stage, 0), (relay_stage, 1), (far_stage, 2), (compute_stage, 3),
        (core_stage, 4), (ring_stage, 5), (return_stage, 6),
    )

    @pl.loop(0, NY + 6)
    def _(s):
        for stage, lag in stages:

            @pl.when(jnp.logical_and(s >= lag, s < NY + lag))
            def _():
                stage(s - lag)

    back_recv[0:PAD, :] = back_send[0:PAD, :]
    lane = iota((TOK, 128), 1)
    named = jnp.zeros((TOK, 128), F32)
    for k in range(TOP):
        named = named + jnp.where(ids[:, k : k + 1] == lane, 1.0, 0.0)
    earlier = onehot(iota((TOK, TOK), 1) < iota((TOK, TOK), 0))
    rank = mm(earlier, named.astype(BF16), ((1,), (0,)))

    @pl.loop(1, NE)
    def _(rel):
        back_copy(rel).wait_recv()

    arrived = back_recv[...]
    total = mm(chosen[0], arrived, ((0,), (0,))) + mm(chosen[1], arrived, ((0,), (0,)))
    gi_out[...] = total[0:TOK, :].astype(BF16)
    wide = iota((TOK, NE * PAD), 1)
    gates = arrived[:, 0:128]
    for k in range(TOP):
        expert = ids[:, k : k + 1]
        position = jnp.sum(jnp.where(expert == lane, rank, 0.0), axis=1, keepdims=True)
        rel = (((expert >> 3) - y) & 3) * NZ + (((expert & 7) - z) & 7)
        line = mm(onehot(wide == rel * PAD + CAP), gates, ((1,), (0,)))
        spot = ((rel & 7) * CAP).astype(F32) + position
        gg_out[:, k : k + 1] = jnp.sum(
            jnp.where(lane.astype(F32) == spot, line, 0.0), axis=1, keepdims=True
        ).astype(BF16)

    @pl.loop(1, NE)
    def _(rel):
        out_copy(rel).wait_send()
        back_copy(rel).wait_send()

    @pl.loop(0, NY)
    def _(c):
        for k in range(8):
            gather_copy(c, k).wait_send()
            sum_copy(c, k).wait_send()
        rows_copy(c).wait()


def weight_grads(hid, rows, grad_in, grad_down):
    x_rows = rows[0]
    grad_in[0, 0] = mm(hid[0], x_rows, ((0,), (0,))).astype(BF16)
    grad_in[0, 1] = mm(hid[1], x_rows, ((0,), (0,))).astype(BF16)
    grad_down[0] = mm(hid[2], rows[1], ((0,), (0,))).astype(BF16)


def on_device(
    token_codes, token_scale, grad_out, expert_ids, gate_probs, w_in, w_in_scale, w_down, w_down_scale
):
    ids_t = jnp.pad(expert_ids.T, ((0, 0), (0, 128 - TOK)), constant_values=-1)
    prob_t = jnp.pad(gate_probs.T, ((0, 0), (0, 128 - TOK)))
    vmem = pl.BlockSpec(memory_space=pltpu.VMEM)
    hbm = pl.BlockSpec(memory_space=pl.ANY)
    dma = pltpu.SemaphoreType.DMA
    grad_input, grad_gates, hid, rows = pl.pallas_call(
        exchange,
        out_shape=(
            jax.ShapeDtypeStruct((TOK, WL), BF16),
            jax.ShapeDtypeStruct((TOK, TOP), BF16),
            jax.ShapeDtypeStruct((3, ROWS, HID), BF16),
            jax.ShapeDtypeStruct((2, ROWS, WIDTH), BF16),
        ),
        in_specs=[vmem] * 8 + [hbm] * 2,
        out_specs=(vmem, vmem, vmem, hbm),
        scratch_shapes=[
            pltpu.VMEM((NE * PAD, 2 * WL), BF16),
            pltpu.VMEM((NE * PAD, 2 * WL), BF16),
            pltpu.VMEM((2, ROWS, WL), BF16),
            pltpu.VMEM((2, ROWS, WIDTH), BF16),
            pltpu.VMEM((3 * HID, WIDTH), BF16),
            pltpu.VMEM((NY, RS, WIDTH), BF16),
            pltpu.VMEM((4, NY, RS, WL), BF16),
            pltpu.VMEM((NY, RS, WL), BF16),
            pltpu.VMEM((NY, RS, WL), BF16),
            pltpu.VMEM((NY, RS, WL), BF16),
            pltpu.VMEM((NY, HALF, WL), BF16),
            pltpu.VMEM((NY, RS - HALF, WL), BF16),
            pltpu.VMEM((NY, RS, WL), BF16),
            pltpu.VMEM((NY, RS, WL), BF16),
            pltpu.VMEM((NE * PAD, WL), BF16),
            pltpu.VMEM((NE * PAD, WL), BF16),
            pltpu.VMEM((2, NE * PAD, 128), BF16),
            pltpu.VMEM((ROWS, 1), F32),
            dma((2,)),
            dma((NY,)),
            dma((NY,)),
            dma((NE,)),
            dma((NE,)),
            dma((8, NY)),
            dma((8, NY)),
            dma((8, NY)),
            dma((8, NY)),
            dma((NE,)),
            dma((NE,)),
        ],
        compiler_params=pltpu.CompilerParams(
            collective_id=0, has_side_effects=True, vmem_limit_bytes=56 * 1024 * 1024
        ),
    )(
        ids_t, prob_t, expert_ids, token_codes, token_scale, grad_out,
        w_in_scale.reshape(2 * HID, WIDTH // BLOCK), w_down_scale.reshape(HID, WIDTH // BLOCK),
        w_in.reshape(2 * HID, WIDTH), w_down.reshape(HID, WIDTH),
    )
    grad_w_in, grad_w_down = pl.pallas_call(
        weight_grads,
        grid=(WIDTH // WL,),
        in_specs=[
            pl.BlockSpec((3, ROWS, HID), lambda i: (0, 0, 0)),
            pl.BlockSpec((2, ROWS, WL), lambda i: (0, 0, i)),
        ],
        out_specs=(
            pl.BlockSpec((1, 2, HID, WL), lambda i: (0, 0, 0, i)),
            pl.BlockSpec((1, HID, WL), lambda i: (0, 0, i)),
        ),
        out_shape=(
            jax.ShapeDtypeStruct((1, 2, HID, WIDTH), BF16),
            jax.ShapeDtypeStruct((1, HID, WIDTH), BF16),
        ),
        compiler_params=pltpu.CompilerParams(vmem_limit_bytes=56 * 1024 * 1024),
    )(hid, rows)
    return (grad_input, grad_gates, grad_w_in, grad_w_down)


def solution(mesh):
    placed = (
        P("expert", "tensor"),
        P("expert", "tensor"),
        P("expert", "tensor"),
        P("expert", None),
        P("expert", None),
        P("expert", None, "tensor", None),
        P("expert", None, "tensor", None),
        P("expert", "tensor", None),
        P("expert", "tensor", None),
    )
    return jax.shard_map(
        on_device,
        mesh=mesh,
        in_specs=placed,
        out_specs=(
            P("expert", "tensor"),
            P("expert", None),
            P("expert", None, "tensor", None),
            P("expert", "tensor", None),
        ),
        check_vma=False,
    )
```

time: 421 us -> 115 us (0.27)
  blocking collectives: 160 us -> 0 us
  Pallas kernels: 0 us -> 102 us
  local copies, waits for them, and re-layouts: 86.5 us -> 10.5 us
  waiting for transfers between devices: 53.5 us -> 0 us
  starting transfers between devices: 42.2 us -> 0 us
  other arithmetic: 36.4 us -> 0 us
  matrix products: 24.6 us -> 0 us
  between operations: 14.5 us -> 0.64 us
    pallas_call x0 -> x2, Pallas kernels: none -> 102 us  [the longest x1 92.6 us: on_device(): pl.pallas_call(exchange, out_shape=(jax.ShapeDtypeStruct((TOK, WL), BF16)...]
    all_to_all x1 -> x0, blocking collectives: 98.4 us -> none  [on_device(): lax.all_to_all(pack_rows(gathered[0]), 'expert', split_axis=1, concat_axi...]
    all_to_all x5 -> x0, waiting for transfers between devices: 53.5 us -> none  [the longest x1 39.9 us: on_device(): lax.all_to_all(pack_rows(gathered[2]), 'expert', split_axis=1, concat_axi...]
    all_to_all x5 -> x0, starting transfers between devices: 42 us -> none  [the longest x1 11.7 us: on_device(): lax.all_to_all(pack_rows(gathered[1]), 'expert', split_axis=1, concat_axi...]
    all_gather x3 -> x0, blocking collectives: 37.9 us -> none  [the longest x1 12.9 us: on_device(): lax.all_gather(grad_blocks, 'tensor', axis=1, tiled=True)]
    mul x8 -> x0, local copies, waits for them, and re-layouts: 27.2 us -> none  [the longest x3 14.4 us: dequant_in(): grouped * w_in_scale[:, :, :, :, None]]
    dot_general x8 -> x0, matrix products: 24.6 us -> none  [the longest x1 5.64 us: on_device(): jnp.einsum('erk,ejfk->ejrf', row_values, w_in_deq, preferred_element_type...]
    unnamed x40 -> x8, local copies, waits for them, and re-layouts: 32.2 us -> 7.89 us
  transfers between devices with their start and end apart: 6 -> 0, of which waited for: 3 -> 0; matrix products, arithmetic and copies ran while one was open for 29% -> 0% of each run, Pallas kernels for 0% -> 0%
where the time goes in v1:
time: 115 us; the launch traced here: 113 us
  Pallas kernels  102 us (89%)
  local copies, waits for them, and re-layouts  10.5 us (9%)
    pallas_call x1, Pallas kernels, on_device(): pl.pallas_call(exchange, out_shape=(jax.ShapeDtypeStruct((TOK, WL), BF16)...  92.6 us
    pallas_call x1, Pallas kernels, on_device(): pl.pallas_call(weight_grads, grid=(WIDTH // WL,), in_specs=[pl.BlockSpec(...  9.69 us
    unnamed x8, local copies, waits for them, and re-layouts  7.89 us

profile of v1, /device:TPU:8, one launch (start us, length us, event | category | flops | bytes accessed | tf_op | source)
XLA Modules:
  0.0 113.4 jit_solution(6817446923317730075)
XLA Ops:
  0.6 1.3 %pad.9.prob_t = f32[8,128]{1,0:T(8,128)} pad(f32[8,32]{1,0:T(8,128)} %bitcast.11, f32[]{:T(128)} %constant.4.clone.1), padding=0_0x0_96 | pad | bytes 5124 | tf_op jit(solution)/shard_map/jit(_pad)/pad | solution.py:380
  1.9 1.3 %pad.8.ids_t = s32[8,128]{1,0:T(8,128)} pad(s32[8,32]{1,0:T(8,128)} %bitcast.10, s32[]{:T(128)} %constant.1.clone.1), padding=0_0x0_96 | pad | bytes 5124 | tf_op jit(solution)/shard_map/jit(_pad)/pad | solution.py:379
  3.2 1.4 %copy.16.tok_scale = bf16[32,5]{1,0:T(8,128)(2,1)} copy(bf16[32,5]{0,1:T(8,128)(2,1)} %param.10) | data formatting | bytes 640 | tf_op args[1]
  4.6 1.4 %copy.15.ids = s32[32,8]{1,0:T(8,128)} copy(s32[32,8]{0,1:T(8,128)} %param.12) | data formatting | bytes 2048 | tf_op args[3]
  5.9 1.5 %copy.14 = f32[1,192,40]{2,1,0:T(8,128)} copy(f32[1,192,40]{1,2,0:T(8,128)} %param.17) | data formatting | bytes 61440 | tf_op args[8]
  7.4 1.7 %copy.13 = f32[1,2,192,40]{3,2,1,0:T(8,128)} copy(f32[1,2,192,40]{2,3,1,0:T(8,128)} %param.15) | data formatting | bytes 122880 | tf_op args[6]
  9.1 92.6 %shard_map.120 = (bf16[32,640]{1,0:T(8,128)(2,1)}, bf16[32,8]{1,0:T(8,128)(2,1)}, bf16[3,384,192]{2,1,0:T(8,128)(2,1)}, bf16[2,384,5120]{2,1,0:T(8,128)(2,1)}) custom-call(s32[8,128]{1,0:T(8,128)} %pad.8.ids_t, f32[8,128]{1,0:T(8,128)} %pad.9.prob_t, s32[32,8]{1,0:T(8,128)} %copy.15.ids, bf16[32,640]{1,0:T(8,128)(2,1)} %codes.1, ...), custom_call_target="tpu_custom_call" | custom-call | tf_op jit(solution)/shard_map/pallas_call | solution.py:384
  101.8 1.3 %copy.17 = bf16[32,8]{0,1:T(8,128)(2,1)} copy(bf16[32,8]{1,0:T(8,128)(2,1)} %get-tuple-element.17) | data formatting | bytes 1024
  103.1 0.0 copy-start
  103.1 9.7 %shard_map.121 = (bf16[1,2,192,5120]{3,2,1,0:T(8,128)(2,1)}, bf16[1,192,5120]{2,1,0:T(8,128)(2,1)}) custom-call(bf16[3,384,192]{2,1,0:T(8,128)(2,1)} %get-tuple-element.12.hid, bf16[2,384,5120]{2,1,0:T(8,128)(2,1)} %get-tuple-element.13.rows), custom_call_target="tpu_custom_call" | custom-call | tf_op jit(solution)/shard_map/pallas_call | solution.py:433
  112.8 0.0 copy-done
  112.8 0.6 copy.19
Async XLA Ops:
  103.1 9.7 %copy-start = (bf16[32,640]{1,0:T(8,128)(2,1)S(1)}, bf16[32,640]{1,0:T(8,128)(2,1)}, u32[]{:S(2)}) copy-start(bf16[32,640]{1,0:T(8,128)(2,1)} %get-tuple-element.24) | copy-start | bytes 122884

commit v2 on v1

v2 whole, which is shorter than its diff:
```python
import functools

import jax
import jax.numpy as jnp
from jax import lax
from jax.experimental import pallas as pl
from jax.experimental.pallas import tpu as pltpu
from jax.sharding import PartitionSpec as P

MESH = pl.DeviceIdType.MESH
BLOCK = 128
CAP = 12
PAD = 16
NX, NY, NZ = 4, 4, 8
NE = NY * NZ
TOK = 32
TOP = 8
WL = 640
WIDTH = 5120
HID = 192
ROWS = NE * CAP
CH = NZ * CAP
CHP = NZ * PAD
HALF = CH // 2
OUT_W = 4 * 256
BACK_W = 4 * 128
RELAYED = (2, 3)
WAY = NZ - 2
STEP = 512
PART = 48
STEPS = 3 * HID // 16 // NY
F32 = jnp.float32
BF16 = jnp.bfloat16


def mm(a, b, dims):
    return lax.dot_general(a, b, (dims, ((), ())), preferred_element_type=F32)


def iota(shape, axis):
    return lax.broadcasted_iota(jnp.int32, shape, axis)


def onehot(mask):
    return jnp.where(mask, 1.0, 0.0).astype(BF16)


def exchange(
    ids_t, prob_t, codes, tok_scale, grad_out, in_scale, down_scale, w_in, w_down,
    gi_out, gg_out, rows, grads,
    payload, scales, send, recv, passing, own, weights, parts, kept_parts, core_in, gate_own, gate_core, gate_chip, gate_in, hid, far_sum, plus_sum, minus_sum,
    relay_a, relay_b, from_minus, from_plus, back_send, back_recv, chosen, gate_pick, gate_spot, prob_col,
    sem_w, sem_own, a_s, a_r, p_s, p_r, g_s, g_r, r_s, r_r, b_s, b_r,
):
    er = lax.axis_index("expert")
    te = lax.axis_index("tensor")
    y, z = lax.div(er, NZ), lax.rem(er, NZ)
    x, core = lax.div(te, 2), lax.rem(te, 2)
    other = 1 - core
    x_plus, x_minus, x_far = lax.rem(x + 1, NX), lax.rem(x + 3, NX), lax.rem(x + 2, NX)
    t_plus, t_minus, t_far = x_plus * 2 + core, x_minus * 2 + core, x_far * 2 + core
    t_core = x * 2 + other

    def ahead(rel):
        dy, dz = lax.div(rel, NZ), lax.rem(rel, NZ)
        return lax.rem(y + dy, NY) * NZ + lax.rem(z + dz, NZ)

    def behind(rel):
        dy, dz = lax.div(rel, NZ), lax.rem(rel, NZ)
        return lax.rem(y + NY - dy, NY) * NZ + lax.rem(z + NZ - dz, NZ)

    barrier = pltpu.get_barrier_semaphore()

    @pl.loop(1, NE)
    def _(rel):
        pl.semaphore_signal(barrier, inc=1, device_id=(ahead(rel), te), device_id_type=MESH)

    for peer in (t_plus, t_minus, t_core, t_far):
        pl.semaphore_signal(barrier, inc=1, device_id=(er, peer), device_id_type=MESH)

    load_in = pltpu.make_async_copy(w_in, weights.at[pl.ds(0, 2 * HID), :], sem_w.at[0])
    load_down = pltpu.make_async_copy(w_down, weights.at[pl.ds(2 * HID, HID), :], sem_w.at[1])
    load_in.start()
    load_down.start()

    eye = onehot(iota((TOK, TOK), 0) == iota((TOK, TOK), 1))
    before = onehot(iota((TOK, TOK), 0) < iota((TOK, TOK), 1))
    tok_cols = mm(eye, tok_scale[...], ((1,), (1,)))
    for j in range(WL // BLOCK):
        cols = slice(j * BLOCK, (j + 1) * BLOCK)
        payload[:, cols] = (codes[:, cols].astype(F32) * tok_cols[:, j : j + 1]).astype(BF16)
    payload[:, WL:] = grad_out[...]

    slot = iota((NE * PAD, TOK), 0)
    rel_of = slot >> 4
    r_of = slot & 15
    expert_of = ((y + (rel_of >> 3)) & 3) * NZ + ((z + (rel_of & 7)) & 7)
    weight = jnp.zeros((NE * PAD, TOK), F32)
    for k in range(TOP):
        weight = weight + jnp.where(ids_t[k : k + 1, :] == expert_of, prob_t[k : k + 1, :], 0.0)
    place = jnp.where(weight > 0.0, mm(onehot(weight > 0.0), before, ((1,), (0,))), -1.0)
    pick = onehot(place == r_of.astype(F32))
    rest_of = jnp.where(jnp.logical_and(r_of >= CAP, r_of < PAD - 1), (r_of - CAP) * 4, -8)
    by_token = jnp.where(r_of == PAD - 1, weight, 0.0).astype(BF16)
    for b in range(4):
        cols = slice(b * 256, (b + 1) * 256)
        packed = mm(pick, payload[:, cols], ((1,), (0,)))
        packed = packed + mm(onehot(place == (rest_of + b).astype(F32)), payload[:, OUT_W:], ((1,), (0,)))
        if b == 0:
            widen = onehot(iota((TOK, 256), 0) == iota((TOK, 256), 1))
            packed = packed + mm(by_token, widen, ((1,), (0,)))
        send[:, cols] = packed.astype(BF16)
    recv[0:PAD, :] = send[0:PAD, :]

    pl.semaphore_wait(barrier, NE - 1 + 4)

    def at16(ref, rel):
        return ref.at[pl.ds(pl.multiple_of(rel * PAD, PAD), PAD), :]

    def out_copy(rel):
        return pltpu.make_async_remote_copy(
            src_ref=at16(send, rel), dst_ref=at16(recv, rel), send_sem=a_s.at[rel], recv_sem=a_r.at[rel],
            device_id=(ahead(rel), te), device_id_type=MESH,
        )

    def pass_copy(dy):
        rel = dy * NZ + NZ // 2
        return pltpu.make_async_remote_copy(
            src_ref=at16(send, rel), dst_ref=passing.at[dy - RELAYED[0]],
            send_sem=a_s.at[rel], recv_sem=p_r.at[dy - RELAYED[0]],
            device_id=(ahead(dy * NZ + WAY), te), device_id_type=MESH,
        )

    def pass_on_copy(dy):
        rel = dy * NZ + NZ // 2
        return pltpu.make_async_remote_copy(
            src_ref=passing.at[dy - RELAYED[0]], dst_ref=at16(recv, rel),
            send_sem=p_s.at[dy - RELAYED[0]], recv_sem=a_r.at[rel],
            device_id=(ahead(WAY), te), device_id_type=MESH,
        )

    def back_copy(rel):
        return pltpu.make_async_remote_copy(
            src_ref=at16(back_send, rel), dst_ref=at16(back_recv, rel), send_sem=b_s.at[rel], recv_sem=b_r.at[rel],
            device_id=(behind(rel), te), device_id_type=MESH,
        )

    def cols_of(t):
        return pl.ds(pl.multiple_of(t * WL, BLOCK), WL)

    def window(c, t, first=0, count=CH):
        return rows.at[:, pl.ds(pl.multiple_of(c * CH + first, 16), count), cols_of(t)]

    def own_rows(c):
        return own.at[:, pl.ds(pl.multiple_of(c * CH, 16), CH), :]

    def own_copy(c):
        return pltpu.make_async_copy(own_rows(c), window(c, te), sem_own.at[c])

    def gather_copy(c, k):
        ref, peer = (
            (lambda: window(c, te), t_plus),
            (lambda: window(c, te), t_minus),
            (lambda: window(c, te), t_core),
            (lambda: window(c, t_minus, 0, HALF), t_plus),
            (lambda: window(c, t_plus, HALF, HALF), t_minus),
            (lambda: window(c, t_minus), t_core),
            (lambda: window(c, t_plus), t_core),
            (lambda: window(c, t_far), t_core),
        )[k]
        ref = ref()
        return pltpu.make_async_remote_copy(
            src_ref=own_rows(c) if k < 3 else ref, dst_ref=ref, send_sem=g_s.at[k, c], recv_sem=g_r.at[k, c],
            device_id=(er, peer), device_id_type=MESH,
        )

    to_core = (x_far * 2 + other, x_plus * 2 + other, x_minus * 2 + other, t_core)

    def sum_copy(c, k):
        if k < 4:
            src, dst, peer = parts.at[k, c], core_in.at[k, c], t_core
        elif k == 4:
            src, dst, peer = far_sum.at[c, pl.ds(0, HALF), :], relay_a.at[c], t_plus
        elif k == 5:
            src, dst, peer = far_sum.at[c, pl.ds(HALF, HALF), :], relay_b.at[c], t_minus
        elif k == 6:
            src, dst, peer = plus_sum.at[c], from_minus.at[c], t_plus
        elif k == 7:
            src, dst, peer = minus_sum.at[c], from_plus.at[c], t_minus
        elif k == 8:
            src, dst, peer = gate_own.at[c], gate_core.at[c], t_core
        else:
            src, dst, peer = gate_chip.at[c], gate_in.at[k - 9, c], (t_plus, t_minus, t_far)[k - 9]
        return pltpu.make_async_remote_copy(
            src_ref=src, dst_ref=dst, send_sem=r_s.at[k, c], recv_sem=r_r.at[k, c],
            device_id=(er, peer), device_id_type=MESH,
        )

    def scales_stage():
        load_in.wait()
        load_down.wait()

        flip = onehot(iota((WIDTH // BLOCK, WIDTH // BLOCK), 0) == iota((WIDTH // BLOCK, WIDTH // BLOCK), 1))
        for part in range(3):
            left = in_scale[part * 40 : (part + 1) * 40, :] if part < 2 else down_scale[...]
            total = jnp.zeros((HID, WIDTH // BLOCK), F32)
            for _ in range(3):
                piece = left.astype(BF16)
                total = total + mm(piece, flip, ((0,), (0,)))
                left = left - piece.astype(F32)
            scales[part * HID : (part + 1) * HID, :] = total

    def scale_stage(c):
        @pl.loop(c * STEPS, (c + 1) * STEPS)
        def _(i):
            at = pl.ds(pl.multiple_of(i * 16, 16), 16)
            scale = scales[at, :]
            for q in range(WIDTH // BLOCK):
                cols = slice(q * BLOCK, (q + 1) * BLOCK)
                weights[at, cols] = (weights[at, cols].astype(F32) * scale[:, q : q + 1]).astype(BF16)

    def prepare_stage():
        ids_col = mm(eye, ids_t[...].astype(F32).astype(BF16), ((1,), (1,))).astype(jnp.int32)
        left = prob_t[...]
        prob_by_token = jnp.zeros((TOK, TOP), F32)
        for _ in range(3):
            piece = left.astype(BF16)
            prob_by_token = prob_by_token + mm(eye, piece, ((1,), (1,)))
            left = left - piece.astype(F32)
        wide = iota((TOK, NE * PAD), 1)
        wide_rel = wide >> 4
        wide_r = wide & 15
        wide_expert = ((y + (wide_rel >> 3)) & 3) * NZ + ((z + (wide_rel & 7)) & 7)
        weight = jnp.zeros((TOK, NE * PAD), F32)
        for k in range(TOP):
            weight = weight + jnp.where(ids_col[:, k : k + 1] == wide_expert, prob_by_token[:, k : k + 1], 0.0)
        earlier = onehot(iota((TOK, TOK), 1) < iota((TOK, TOK), 0))
        place = jnp.where(weight > 0.0, mm(earlier, onehot(weight > 0.0), ((1,), (0,))), -1.0)
        rest = jnp.where(jnp.logical_and(wide_r >= CAP, wide_r < PAD - 1), (wide_r - CAP) * 4, -8)
        for b in range(5):
            here = wide_r if b == 4 else rest + b
            kept = jnp.where(place == here.astype(F32), weight, 0.0)
            high = kept.astype(BF16)
            chosen[b, 0:TOK, :] = high
            chosen[b, TOK:, :] = (kept - high.astype(F32)).astype(BF16)
        lane = iota((TOK, 128), 1)
        for k in range(TOP):
            expert = ids_col[:, k : k + 1]
            rel = (((expert >> 3) - y) & 3) * NZ + (((expert & 7) - z) & 7)
            row = wide == rel * PAD + PAD - 1
            gate_pick[k * TOK : (k + 1) * TOK, :] = onehot(row)
            position = jnp.sum(jnp.where(row, place, 0.0), axis=1, keepdims=True)
            spot = ((rel & 7) * CAP).astype(F32) + position
            gate_spot[k * TOK : (k + 1) * TOK, :] = onehot(lane.astype(F32) == spot)

    def send_stage(c):
        @pl.loop(0, NZ)
        def _(i):
            rel = c * NZ + i
            relayed = jnp.logical_and(rel >= RELAYED[0] * NZ, i == NZ // 2)

            @pl.when(jnp.logical_and(rel > 0, jnp.logical_not(relayed)))
            def _():
                out_copy(rel).start()

        for dy in RELAYED:

            @pl.when(c == dy - 1)
            def _():
                pass_copy(dy).start()

    def sent_stage(c):
        @pl.loop(0, NZ)
        def _(i):
            rel = c * NZ + i
            relayed = jnp.logical_and(rel >= RELAYED[0] * NZ, i == NZ // 2)

            @pl.when(jnp.logical_and(rel > 0, jnp.logical_not(relayed)))
            def _():
                out_copy(rel).wait_send()

    send_stage(0)

    def dispatch_stage(c):
        sent_stage(c)

        @pl.when(c < NY - 1)
        def _():
            send_stage(c + 1)

        @pl.loop(0, NZ)
        def _(i):
            rel = c * NZ + i

            @pl.when(rel > 0)
            def _():
                out_copy(rel).wait_recv()

        row = iota((CH, CHP), 0)
        col = iota((CH, CHP), 1)
        group = lax.div(row, CAP)
        within = row - group * CAP
        squeeze = onehot(col == group * PAD + within)
        span = pl.ds(pl.multiple_of(c * CH, 16), CH)
        part = pl.ds(pl.multiple_of(c * CHP, CHP), CHP)
        own[0, span, :] = mm(squeeze, recv[part, :WL], ((1,), (0,))).astype(BF16)
        own[1, span, 0 : OUT_W - WL] = mm(squeeze, recv[part, WL:OUT_W], ((1,), (0,))).astype(BF16)
        rest = jnp.zeros((CH, 256), F32)
        for b in range(4):
            here = jnp.logical_and(col == group * PAD + CAP + (within >> 2), (within & 3) == b)
            rest = rest + mm(onehot(here), recv[part, b * 256 : (b + 1) * 256], ((1,), (0,)))
        own[1, span, OUT_W - WL :] = rest.astype(BF16)
        own_copy(c).start()
        for k in (0, 1, 2):
            gather_copy(c, k).start()
        named = mm(onehot(col == group * PAD + PAD - 1), recv[part, :BLOCK], ((1,), (0,)))[:, :TOK]
        rank = mm(onehot(named > 0.0), before, ((1,), (0,)))
        taken = jnp.logical_and(named > 0.0, rank == within[:, :TOK].astype(F32))
        prob_col[span, :] = jnp.sum(jnp.where(taken, named, 0.0), axis=1, keepdims=True)

        for dy in RELAYED:

            @pl.when(c == dy - 1)
            def _():
                pass_copy(dy).wait_recv()
                pass_on_copy(dy).start()

        @pl.when(c == 0)
        def _():
            scales_stage()

        scale_stage(c)

    def relay_stage(c):
        gather_copy(c, 0).wait_recv()
        gather_copy(c, 3).start()
        gather_copy(c, 5).start()
        gather_copy(c, 1).wait_recv()
        gather_copy(c, 4).start()
        gather_copy(c, 6).start()

    def far_stage(c):
        gather_copy(c, 3).wait_recv()
        gather_copy(c, 4).wait_recv()
        gather_copy(c, 7).start()

    def compute_stage(c):
        for k in (2, 5, 6, 7):
            gather_copy(c, k).wait_recv()
        own_copy(c).wait()
        span = pl.ds(pl.multiple_of(c * CH, 16), CH)
        row_values = rows[0, span, :]
        gate = mm(row_values, weights[0:HID, :], ((1,), (1,)))
        up = mm(row_values, weights[HID : 2 * HID, :], ((1,), (1,)))
        hidden = mm(rows[1, span, :], weights[2 * HID :, :], ((1,), (1,)))
        sig = jax.nn.sigmoid(gate)
        act = gate * sig
        gate_full = hidden * up * sig * (1.0 + gate * (1.0 - sig))
        up_full = hidden * act
        gate_grad = gate_full.astype(BF16)
        up_grad = up_full.astype(BF16)
        acted = act * up
        for k in range(8):
            t = (to_core + (t_far, t_plus, t_minus, te))[k]
            part = mm(gate_grad, weights[0:HID, cols_of(t)], ((1,), (0,)))
            part = part + mm(up_grad, weights[HID : 2 * HID, cols_of(t)], ((1,), (0,)))
            if k < 4:
                parts[k, c] = part.astype(BF16)
                sum_copy(c, k).start()
            else:
                kept_parts[k - 4, c] = part.astype(BF16)
        share = hidden * acted
        ones = jnp.ones((8, HID), BF16)
        gate_row = jnp.zeros((8, CH), F32)
        for _ in range(3):
            piece = share.astype(BF16)
            gate_row = gate_row + mm(ones, piece, ((1,), (1,)))
            share = share - piece.astype(F32)
        gate_own[c] = jnp.concatenate([gate_row, jnp.zeros((8, 128 - CH), F32)], axis=1)
        sum_copy(c, 8).start()
        prob = prob_col[span, :]
        hid[0, span, :] = (prob * gate_full).astype(BF16)
        hid[1, span, :] = (prob * up_full).astype(BF16)
        hid[2, span, :] = (prob * acted).astype(BF16)

    def chip_sum(c, k):
        return kept_parts[k, c].astype(F32) + core_in[k, c].astype(F32)

    def core_stage(c):
        sum_copy(c, 0).wait_recv()
        far_sum[c] = chip_sum(c, 0).astype(BF16)
        sum_copy(c, 4).start()
        sum_copy(c, 5).start()
        sum_copy(c, 8).wait_recv()
        gate_chip[c] = gate_own[c] + gate_core[c]
        for k in (9, 10, 11):
            sum_copy(c, k).start()

    def ring_stage(c):
        sum_copy(c, 1).wait_recv()
        total = chip_sum(c, 1)
        sum_copy(c, 4).wait_recv()
        plus_sum[c, 0:HALF, :] = (total[0:HALF] + relay_a[c].astype(F32)).astype(BF16)
        plus_sum[c, HALF:CH, :] = total[HALF:CH].astype(BF16)
        sum_copy(c, 6).start()
        sum_copy(c, 2).wait_recv()
        total = chip_sum(c, 2)
        sum_copy(c, 5).wait_recv()
        minus_sum[c, 0:HALF, :] = total[0:HALF].astype(BF16)
        minus_sum[c, HALF:CH, :] = (total[HALF:CH] + relay_b[c].astype(F32)).astype(BF16)
        sum_copy(c, 7).start()

    def return_stage(c):
        sum_copy(c, 3).wait_recv()
        total = chip_sum(c, 3)
        sum_copy(c, 6).wait_recv()
        sum_copy(c, 7).wait_recv()
        for k in (9, 10, 11):
            sum_copy(c, k).wait_recv()
        gate_row = (gate_chip[c] + gate_in[2, c]) + (gate_in[0, c] + gate_in[1, c])
        total = total + from_minus[c].astype(F32) + from_plus[c].astype(F32)
        row = iota((CHP, CH), 0)
        col = iota((CHP, CH), 1)
        r = row & 15
        first = (row >> 4) * CAP
        spread = onehot(jnp.logical_and(r < CAP, col == first + r))
        extra = jnp.logical_and(r >= CAP, r < PAD - 1)
        values = total.astype(BF16)
        at = pl.ds(pl.multiple_of(c * CHP, CHP), CHP)
        for b in range(4):
            out = mm(spread, values[:, b * 128 : (b + 1) * 128], ((1,), (0,)))
            there = onehot(jnp.logical_and(extra, col == first + (r - CAP) * 4 + b))
            out = out + mm(there, values[:, BACK_W:], ((1,), (0,)))
            if b == 0:
                out = out + jnp.where(iota((CHP, 128), 0) & 15 == PAD - 1, gate_row[0:1, :], 0.0)
            back_send[at, b * 128 : (b + 1) * 128] = out.astype(BF16)

        @pl.loop(0, NZ)
        def _(i):
            rel = c * NZ + i

            @pl.when(rel > 0)
            def _():
                back_copy(rel).start()

    stages = (
        (dispatch_stage, 0), (relay_stage, 1), (far_stage, 2), (compute_stage, 3),
        (core_stage, 4), (ring_stage, 5), (return_stage, 6),
    )

    @pl.loop(0, NY + 6)
    def _(s):
        for stage, lag in stages:

            @pl.when(jnp.logical_and(s >= lag, s < NY + lag))
            def _():
                stage(s - lag)

        @pl.when(s == NY)
        def _():
            prepare_stage()

        for k in range(3):

            @pl.when(s == NY + 2 + k)
            def _():
                turned = hid[k].T
                for i in range(WIDTH // STEP):
                    cols = slice(i * STEP, (i + 1) * STEP)
                    grads[k, :, cols] = mm(turned, rows[k // 2, :, cols], ((1,), (0,))).astype(BF16)

    back_recv[0:PAD, :] = back_send[0:PAD, :]
    @pl.loop(1, NE)
    def _(rel):
        back_copy(rel).wait_recv()

    total = mm(chosen[4], back_recv[...], ((1,), (0,)))
    gi_out[:, 0:BACK_W] = (total[0:TOK] + total[TOK:]).astype(BF16)
    total = jnp.zeros((2 * TOK, 128), F32)
    for b in range(4):
        total = total + mm(chosen[b], back_recv[:, b * 128 : (b + 1) * 128], ((1,), (0,)))
    gi_out[:, BACK_W:] = (total[0:TOK] + total[TOK:]).astype(BF16)
    line = mm(gate_pick[...], back_recv[:, 0:128], ((1,), (0,)))
    line = (line * gate_spot[...].astype(F32)).astype(BF16)
    line = mm(jnp.ones((TOP, 128), BF16), line, ((1,), (1,)))
    at_k = iota((TOP, TOP * TOK), 1) >> 5 == iota((TOP, TOP * TOK), 0)
    at_t = iota((TOP * TOK, TOK), 0) & 31 == iota((TOP * TOK, TOK), 1)
    gg_out[...] = mm(jnp.where(at_k, line, 0.0).astype(BF16), onehot(at_t), ((1,), (0,))).astype(BF16)

    @pl.loop(1, NE)
    def _(rel):
        back_copy(rel).wait_send()

    for dy in RELAYED:
        pass_copy(dy).wait_send()
        pass_on_copy(dy).wait_send()

    @pl.loop(0, NY)
    def _(c):
        for k in range(8):
            gather_copy(c, k).wait_send()
        for k in range(12):
            sum_copy(c, k).wait_send()


def put_grads(grads, grad_in, grad_down, sems):
    copies = [
        pltpu.make_async_copy(
            grads.at[k, pl.ds(i * PART, PART), :],
            (grad_down.at[0] if k == 2 else grad_in.at[0, k]).at[pl.ds(i * PART, PART), :],
            sems.at[k, i],
        )
        for k in range(3)
        for i in range(HID // PART)
    ]
    for copy in copies:
        copy.start()
    for copy in copies:
        copy.wait()


def on_device(
    token_codes, token_scale, grad_out, expert_ids, gate_probs, w_in, w_in_scale, w_down, w_down_scale
):
    vmem = pl.BlockSpec(memory_space=pltpu.VMEM)
    hbm = pl.BlockSpec(memory_space=pl.ANY)
    dma = pltpu.SemaphoreType.DMA
    grad_input, grad_gates, _, grads = pl.pallas_call(
        exchange,
        out_shape=(
            jax.ShapeDtypeStruct((TOK, WL), BF16),
            jax.ShapeDtypeStruct((TOP, TOK), BF16),
            pltpu.VMEM((2, ROWS, WIDTH), BF16),
            pltpu.VMEM((3, HID, WIDTH), BF16),
        ),
        in_specs=[vmem] * 7 + [hbm] * 2,
        out_specs=(vmem, vmem, vmem, vmem),
        scratch_shapes=[
            pltpu.VMEM((TOK, 2 * WL), BF16),
            pltpu.VMEM((3 * HID, WIDTH // BLOCK), F32),
            pltpu.VMEM((NE * PAD, OUT_W), BF16),
            pltpu.VMEM((NE * PAD, OUT_W), BF16),
            pltpu.VMEM((len(RELAYED), PAD, OUT_W), BF16),
            pltpu.VMEM((2, ROWS, WL), BF16),
            pltpu.VMEM((3 * HID, WIDTH), BF16),
            pltpu.VMEM((4, NY, CH, WL), BF16),
            pltpu.VMEM((4, NY, CH, WL), BF16),
            pltpu.VMEM((4, NY, CH, WL), BF16),
            pltpu.VMEM((NY, 8, 128), F32),
            pltpu.VMEM((NY, 8, 128), F32),
            pltpu.VMEM((NY, 8, 128), F32),
            pltpu.VMEM((3, NY, 8, 128), F32),
            pltpu.VMEM((3, ROWS, HID), BF16),
            pltpu.VMEM((NY, CH, WL), BF16),
            pltpu.VMEM((NY, CH, WL), BF16),
            pltpu.VMEM((NY, CH, WL), BF16),
            pltpu.VMEM((NY, HALF, WL), BF16),
            pltpu.VMEM((NY, HALF, WL), BF16),
            pltpu.VMEM((NY, CH, WL), BF16),
            pltpu.VMEM((NY, CH, WL), BF16),
            pltpu.VMEM((NE * PAD, BACK_W), BF16),
            pltpu.VMEM((NE * PAD, BACK_W), BF16),
            pltpu.VMEM((5, 2 * TOK, NE * PAD), BF16),
            pltpu.VMEM((TOP * TOK, NE * PAD), BF16),
            pltpu.VMEM((TOP * TOK, 128), BF16),
            pltpu.VMEM((ROWS, 1), F32),
            dma((2,)),
            dma((NY,)),
            dma((NE,)),
            dma((NE,)),
            dma((len(RELAYED),)),
            dma((len(RELAYED),)),
            dma((8, NY)),
            dma((8, NY)),
            dma((12, NY)),
            dma((12, NY)),
            dma((NE,)),
            dma((NE,)),
        ],
        compiler_params=pltpu.CompilerParams(
            collective_id=0, has_side_effects=True, vmem_limit_bytes=44 * 1024 * 1024
        ),
    )(
        expert_ids.T, gate_probs.T, token_codes, token_scale.T, grad_out,
        w_in_scale.transpose(0, 1, 3, 2).reshape(2 * (WIDTH // BLOCK), HID),
        w_down_scale.transpose(0, 2, 1).reshape(WIDTH // BLOCK, HID),
        w_in.reshape(2 * HID, WIDTH), w_down.reshape(HID, WIDTH),
    )
    grad_w_in, grad_w_down = pl.pallas_call(
        put_grads,
        in_specs=[vmem],
        out_specs=(hbm, hbm),
        out_shape=(
            jax.ShapeDtypeStruct((1, 2, HID, WIDTH), BF16),
            jax.ShapeDtypeStruct((1, HID, WIDTH), BF16),
        ),
        scratch_shapes=[dma((3, HID // PART))],
        compiler_params=pltpu.CompilerParams(vmem_limit_bytes=8 * 1024 * 1024),
    )(grads)
    return (grad_input, grad_gates.T, grad_w_in, grad_w_down)


def solution(mesh):
    placed = (
        P("expert", "tensor"),
        P("expert", "tensor"),
        P("expert", "tensor"),
        P("expert", None),
        P("expert", None),
        P("expert", None, "tensor", None),
        P("expert", None, "tensor", None),
        P("expert", "tensor", None),
        P("expert", "tensor", None),
    )
    return jax.shard_map(
        on_device,
        mesh=mesh,
        in_specs=placed,
        out_specs=(
            P("expert", "tensor"),
            P("expert", None),
            P("expert", None, "tensor", None),
            P("expert", "tensor", None),
        ),
        check_vma=False,
    )
```

time: 115 us -> 97.7 us (0.85); the launches traced: 113 us -> 97.5 us
  local copies, waits for them, and re-layouts: 10.5 us -> 1.21 us
  Pallas kernels: 102 us -> 95.7 us
    pallas_call x1, Pallas kernels: 9.69 us -> 2.64 us  [on_device(): pl.pallas_call(put_grads, in_specs=[vmem], out_specs=(hbm, hbm), out_shap...]
    unnamed x8 -> x6, local copies, waits for them, and re-layouts: 7.89 us -> 1.21 us
    pad x2 -> x0, local copies, waits for them, and re-layouts: 2.56 us -> none  [the longest x1 1.28 us: on_device(): ids_t = jnp.pad(expert_ids.T, ((0, 0), (0, 128 - TOK)), constant_values=-1)]
where the time goes in v2:
time: 97.7 us; the launch traced here: 97.5 us
  Pallas kernels  95.7 us (98%)
  local copies, waits for them, and re-layouts  1.21 us (1%)
    pallas_call x1, Pallas kernels, on_device(): pl.pallas_call(exchange, out_shape=(jax.ShapeDtypeStruct((TOK, WL), BF16)...  93 us
    pallas_call x1, Pallas kernels, on_device(): pl.pallas_call(put_grads, in_specs=[vmem], out_specs=(hbm, hbm), out_shap...  2.64 us

profile of v2, /device:TPU:8, one launch (start us, length us, event | category | flops | bytes accessed | tf_op | source)
XLA Modules:
  0.0 97.5 jit_solution(11363999101143727467)
XLA Ops:
  0.6 93.0 %shard_map.120 = (bf16[32,640]{1,0:T(8,128)(2,1)}, bf16[8,32]{1,0:T(8,128)(2,1)}, bf16[2,384,5120]{2,1,0:T(8,128)(2,1)}, bf16[3,192,5120]{2,1,0:T(8,128)(2,1)S(1)}) custom-call(s32[8,32]{1,0:T(8,128)} %bitcast.16, f32[8,32]{1,0:T(8,128)} %bitcast.17, bf16[32,640]{1,0:T(8,128)(2,1)} %codes.1, bf16[5,32]{1,0:T(8,128)(2,1)} %bitcast.18, ...), custom_call_target="tpu_custom_call" | custom-call | tf_op jit(solution)/shard_map/pallas_call | solution.py:528
  93.7 0.0 copy-start
  93.7 0.0 copy-start.1
  93.7 2.6 %shard_map.121 = (bf16[1,2,192,5120]{3,2,1,0:T(8,128)(2,1)}, bf16[1,192,5120]{2,1,0:T(8,128)(2,1)}) custom-call(bf16[3,192,5120]{2,1,0:T(8,128)(2,1)S(1)} %get-tuple-element.11.grads), custom_call_target="tpu_custom_call" | custom-call | tf_op jit(solution)/shard_map/pallas_call | solution.py:589
  96.3 0.0 copy-done
  96.3 0.6 copy.15
  97.0 0.0 copy-done.1
  97.0 0.6 copy.16
Async XLA Ops:
  93.7 2.7 %copy-start = (bf16[32,640]{1,0:T(8,128)(2,1)S(1)}, bf16[32,640]{1,0:T(8,128)(2,1)}, u32[]{:S(2)}) copy-start(bf16[32,640]{1,0:T(8,128)(2,1)} %get-tuple-element.18) | copy-start | bytes 122884
  93.7 3.3 %copy-start.1 = (bf16[8,32]{1,0:T(8,128)(2,1)S(1)}, bf16[8,32]{1,0:T(8,128)(2,1)}, u32[]{:S(2)}) copy-start(bf16[8,32]{1,0:T(8,128)(2,1)} %get-tuple-element.10) | copy-start | bytes 1540

commit v3 on v2

--- a/solution.py
+++ b/solution.py
@@ -46,11 +46,12 @@
 
 
 def exchange(
-    ids_t, prob_t, codes, tok_scale, grad_out, in_scale, down_scale, w_in, w_down,
-    gi_out, gg_out, rows, grads,
+    ids_hbm, prob_hbm, codes_hbm, tok_scale_hbm, grad_hbm, in_scale_hbm, down_scale_hbm, w_in, w_down,
+    gi_out, gg_out, grads, rows,
+    ids_t, prob_t, codes, tok_scale, grad_out, in_scale, down_scale,
     payload, scales, send, recv, passing, own, weights, parts, kept_parts, core_in, gate_own, gate_core, gate_chip, gate_in, hid, far_sum, plus_sum, minus_sum,
     relay_a, relay_b, from_minus, from_plus, back_send, back_recv, chosen, gate_pick, gate_spot, prob_col,
-    sem_w, sem_own, a_s, a_r, p_s, p_r, g_s, g_r, r_s, r_r, b_s, b_r,
+    sem_in, sem_w, sem_own, a_s, a_r, p_s, p_r, g_s, g_r, r_s, r_r, b_s, b_r,
 ):
     er = lax.axis_index("expert")
     te = lax.axis_index("tensor")
@@ -78,10 +79,23 @@
     for peer in (t_plus, t_minus, t_core, t_far):
         pl.semaphore_signal(barrier, inc=1, device_id=(er, peer), device_id_type=MESH)
 
+    loads = [
+        pltpu.make_async_copy(src, dst, sem_in.at[i])
+        for i, (src, dst) in enumerate(
+            (
+                (ids_hbm, ids_t), (prob_hbm, prob_t), (codes_hbm, codes), (tok_scale_hbm, tok_scale),
+                (grad_hbm, grad_out), (in_scale_hbm, in_scale), (down_scale_hbm, down_scale),
+            )
+        )
+    ]
+    for load in loads:
+        load.start()
     load_in = pltpu.make_async_copy(w_in, weights.at[pl.ds(0, 2 * HID), :], sem_w.at[0])
     load_down = pltpu.make_async_copy(w_down, weights.at[pl.ds(2 * HID, HID), :], sem_w.at[1])
     load_in.start()
     load_down.start()
+    for load in loads[:5]:
+        load.wait()
 
     eye = onehot(iota((TOK, TOK), 0) == iota((TOK, TOK), 1))
     before = onehot(iota((TOK, TOK), 0) < iota((TOK, TOK), 1))
@@ -197,6 +211,8 @@
         )
 
     def scales_stage():
+        for load in loads[5:]:
+            load.wait()
         load_in.wait()
         load_down.wait()
 
@@ -470,8 +486,20 @@
                     grads[k, :, cols] = mm(turned, rows[k // 2, :, cols], ((1,), (0,))).astype(BF16)
 
     back_recv[0:PAD, :] = back_send[0:PAD, :]
+    for dy in RELAYED:
+        pass_copy(dy).wait_send()
+        pass_on_copy(dy).wait_send()
+
+    @pl.loop(0, NY)
+    def _(c):
+        for k in range(8):
+            gather_copy(c, k).wait_send()
+        for k in range(12):
+            sum_copy(c, k).wait_send()
+
     @pl.loop(1, NE)
     def _(rel):
+        back_copy(rel).wait_send()
         back_copy(rel).wait_recv()
 
     total = mm(chosen[4], back_recv[...], ((1,), (0,)))
@@ -487,23 +515,8 @@
     at_t = iota((TOP * TOK, TOK), 0) & 31 == iota((TOP * TOK, TOK), 1)
     gg_out[...] = mm(jnp.where(at_k, line, 0.0).astype(BF16), onehot(at_t), ((1,), (0,))).astype(BF16)
 
-    @pl.loop(1, NE)
-    def _(rel):
-        back_copy(rel).wait_send()
-
-    for dy in RELAYED:
-        pass_copy(dy).wait_send()
-        pass_on_copy(dy).wait_send()
-
-    @pl.loop(0, NY)
-    def _(c):
-        for k in range(8):
-            gather_copy(c, k).wait_send()
-        for k in range(12):
-            sum_copy(c, k).wait_send()
-
-
-def put_grads(grads, grad_in, grad_down, sems):
+
+def put_grads(grads, gi, gg, grad_in, grad_down, gi_out, gg_out, sems, small):
     copies = [
         pltpu.make_async_copy(
             grads.at[k, pl.ds(i * PART, PART), :],
@@ -513,6 +526,7 @@
         for k in range(3)
         for i in range(HID // PART)
     ]
+    copies += [pltpu.make_async_copy(gi, gi_out, small.at[0]), pltpu.make_async_copy(gg, gg_out, small.at[1])]
     for copy in copies:
         copy.start()
     for copy in copies:
@@ -525,17 +539,24 @@
     vmem = pl.BlockSpec(memory_space=pltpu.VMEM)
     hbm = pl.BlockSpec(memory_space=pl.ANY)
     dma = pltpu.SemaphoreType.DMA
-    grad_input, grad_gates, _, grads = pl.pallas_call(
+    input_sum, gate_sum, grads = pl.pallas_call(
         exchange,
         out_shape=(
-            jax.ShapeDtypeStruct((TOK, WL), BF16),
-            jax.ShapeDtypeStruct((TOP, TOK), BF16),
-            pltpu.VMEM((2, ROWS, WIDTH), BF16),
+            pltpu.VMEM((TOK, WL), BF16),
+            pltpu.VMEM((TOP, TOK), BF16),
             pltpu.VMEM((3, HID, WIDTH), BF16),
         ),
-        in_specs=[vmem] * 7 + [hbm] * 2,
-        out_specs=(vmem, vmem, vmem, vmem),
+        in_specs=[hbm] * 9,
+        out_specs=(vmem, vmem, vmem),
         scratch_shapes=[
+            pltpu.VMEM((2, ROWS, WIDTH), BF16),
+            pltpu.VMEM((TOP, TOK), jnp.int32),
+            pltpu.VMEM((TOP, TOK), F32),
+            pltpu.VMEM((TOK, WL), BF16),
+            pltpu.VMEM((WL // BLOCK, TOK), BF16),
+            pltpu.VMEM((TOK, WL), BF16),
+            pltpu.VMEM((2 * (WIDTH // BLOCK), HID), F32),
+            pltpu.VMEM((WIDTH // BLOCK, HID), F32),
             pltpu.VMEM((TOK, 2 * WL), BF16),
             pltpu.VMEM((3 * HID, WIDTH // BLOCK), F32),
             pltpu.VMEM((NE * PAD, OUT_W), BF16),
@@ -564,6 +585,7 @@
             pltpu.VMEM((TOP * TOK, NE * PAD), BF16),
             pltpu.VMEM((TOP * TOK, 128), BF16),
             pltpu.VMEM((ROWS, 1), F32),
+            dma((7,)),
             dma((2,)),
             dma((NY,)),
             dma((NE,)),
@@ -578,7 +600,7 @@
             dma((NE,)),
         ],
         compiler_params=pltpu.CompilerParams(
-            collective_id=0, has_side_effects=True, vmem_limit_bytes=44 * 1024 * 1024
+            collective_id=0, has_side_effects=True, vmem_limit_bytes=52 * 1024 * 1024
         ),
     )(
         expert_ids.T, gate_probs.T, token_codes, token_scale.T, grad_out,
@@ -586,17 +608,19 @@
         w_down_scale.transpose(0, 2, 1).reshape(WIDTH // BLOCK, HID),
         w_in.reshape(2 * HID, WIDTH), w_down.reshape(HID, WIDTH),
     )
-    grad_w_in, grad_w_down = pl.pallas_call(
+    grad_w_in, grad_w_down, grad_input, grad_gates = pl.pallas_call(
         put_grads,
-        in_specs=[vmem],
-        out_specs=(hbm, hbm),
+        in_specs=[vmem] * 3,
+        out_specs=(hbm,) * 4,
         out_shape=(
             jax.ShapeDtypeStruct((1, 2, HID, WIDTH), BF16),
             jax.ShapeDtypeStruct((1, HID, WIDTH), BF16),
+            jax.ShapeDtypeStruct((TOK, WL), BF16),
+            jax.ShapeDtypeStruct((TOP, TOK), BF16),
         ),
-        scratch_shapes=[dma((3, HID // PART))],
+        scratch_shapes=[dma((3, HID // PART)), dma((2,))],
         compiler_params=pltpu.CompilerParams(vmem_limit_bytes=8 * 1024 * 1024),
-    )(grads)
+    )(grads, input_sum, gate_sum)
     return (grad_input, grad_gates.T, grad_w_in, grad_w_down)
 
 

time: 97.7 us -> 93.3 us (0.955)
  Pallas kernels: 95.7 us -> 92.5 us
  local copies, waits for them, and re-layouts: 1.21 us -> 0 us
    pallas_call x2, Pallas kernels: 95.7 us -> 92.5 us  [the longest x1 89.8 us: on_device(): pl.pallas_call(exchange, out_shape=(pltpu.VMEM((TOK, WL), BF16), pltpu.VM...]
    unnamed x6 -> x0, local copies, waits for them, and re-layouts: 1.21 us -> none
where the time goes in v3:
time: 93.3 us; the launch traced here: 93.2 us
  Pallas kernels  92.5 us (99%)
    pallas_call x1, Pallas kernels, on_device(): pl.pallas_call(exchange, out_shape=(pltpu.VMEM((TOK, WL), BF16), pltpu.VM...  89.8 us
    pallas_call x1, Pallas kernels, on_device(): pl.pallas_call(put_grads, in_specs=[vmem] * 3, out_specs=(hbm,) * 4, out_...  2.67 us

profile of v3, /device:TPU:8, one launch (start us, length us, event | category | flops | bytes accessed | tf_op | source)
XLA Modules:
  0.0 93.2 jit_solution(9384188089364461482)
XLA Ops:
  0.6 89.8 %shard_map.120 = (bf16[32,640]{1,0:T(8,128)(2,1)S(1)}, bf16[8,32]{1,0:T(8,128)(2,1)S(1)}, bf16[3,192,5120]{2,1,0:T(8,128)(2,1)S(1)}) custom-call(s32[8,32]{1,0:T(8,128)} %bitcast.16, f32[8,32]{1,0:T(8,128)} %bitcast.17, bf16[32,640]{1,0:T(8,128)(2,1)} %codes_hbm.1, bf16[5,32]{1,0:T(8,128)(2,1)} %bitcast.18, bf16[32,640]{1,0:T(8,128)(2,1)} %grad_hbm.1, ...), custom_call_target="tpu_custom_call" | custom-call | tf_op jit(solution)/shard_map/pallas_call | solution.py:542
  90.5 2.7 %shard_map.121 = (bf16[1,2,192,5120]{3,2,1,0:T(8,128)(2,1)}, bf16[1,192,5120]{2,1,0:T(8,128)(2,1)}, bf16[32,640]{1,0:T(8,128)(2,1)}, bf16[8,32]{1,0:T(8,128)(2,1)}) custom-call(bf16[3,192,5120]{2,1,0:T(8,128)(2,1)S(1)} %get-tuple-element.11.grads, bf16[32,640]{1,0:T(8,128)(2,1)S(1)} %get-tuple-element.12.gi, bf16[8,32]{1,0:T(8,128)(2,1)S(1)} %get-tuple-element.13.gg), custom_call_target="tpu_custom_call" | custom-call | tf_op jit(solution)/shard_map/pallas_call | solution.py:611

commit v4 on v3

--- a/solution.py
+++ b/solution.py
@@ -269,11 +269,15 @@
             spot = ((rel & 7) * CAP).astype(F32) + position
             gate_spot[k * TOK : (k + 1) * TOK, :] = onehot(lane.astype(F32) == spot)
 
+    def far_first(c, i):
+        half = i // 2
+        return c * NZ + (NZ // 2 + half - (i % 2) * (2 * half + 1) + NZ) % NZ
+
     def send_stage(c):
         @pl.loop(0, NZ)
         def _(i):
-            rel = c * NZ + i
-            relayed = jnp.logical_and(rel >= RELAYED[0] * NZ, i == NZ // 2)
+            rel = far_first(c, i)
+            relayed = jnp.logical_and(rel >= RELAYED[0] * NZ, lax.rem(rel, NZ) == NZ // 2)
 
             @pl.when(jnp.logical_and(rel > 0, jnp.logical_not(relayed)))
             def _():
@@ -453,7 +457,7 @@
 
         @pl.loop(0, NZ)
         def _(i):
-            rel = c * NZ + i
+            rel = far_first(c, i)
 
             @pl.when(rel > 0)
             def _():

time: 93.3 us -> 92.6 us (level)
  no operation moved by 1% of the time
where the time goes in v4:
time: 92.6 us; the launch traced here: 92.5 us
  Pallas kernels  91.8 us (99%)
    pallas_call x1, Pallas kernels, on_device(): pl.pallas_call(exchange, out_shape=(pltpu.VMEM((TOK, WL), BF16), pltpu.VM...  89.1 us
    pallas_call x1, Pallas kernels, on_device(): pl.pallas_call(put_grads, in_specs=[vmem] * 3, out_specs=(hbm,) * 4, out_...  2.67 us

profile of v4, /device:TPU:8, one launch (start us, length us, event | category | flops | bytes accessed | tf_op | source)
XLA Modules:
  0.0 92.5 jit_solution(12525633428957993333)
XLA Ops:
  0.6 89.1 %shard_map.120 = (bf16[32,640]{1,0:T(8,128)(2,1)S(1)}, bf16[8,32]{1,0:T(8,128)(2,1)S(1)}, bf16[3,192,5120]{2,1,0:T(8,128)(2,1)S(1)}) custom-call(s32[8,32]{1,0:T(8,128)} %bitcast.16, f32[8,32]{1,0:T(8,128)} %bitcast.17, bf16[32,640]{1,0:T(8,128)(2,1)} %codes_hbm.1, bf16[5,32]{1,0:T(8,128)(2,1)} %bitcast.18, bf16[32,640]{1,0:T(8,128)(2,1)} %grad_hbm.1, ...), custom_call_target="tpu_custom_call" | custom-call | tf_op jit(solution)/shard_map/pallas_call | solution.py:546
  89.8 2.7 %shard_map.121 = (bf16[1,2,192,5120]{3,2,1,0:T(8,128)(2,1)}, bf16[1,192,5120]{2,1,0:T(8,128)(2,1)}, bf16[32,640]{1,0:T(8,128)(2,1)}, bf16[8,32]{1,0:T(8,128)(2,1)}) custom-call(bf16[3,192,5120]{2,1,0:T(8,128)(2,1)S(1)} %get-tuple-element.11.grads, bf16[32,640]{1,0:T(8,128)(2,1)S(1)} %get-tuple-element.12.gi, bf16[8,32]{1,0:T(8,128)(2,1)S(1)} %get-tuple-element.13.gg), custom_call_target="tpu_custom_call" | custom-call | tf_op jit(solution)/shard_map/pallas_call | solution.py:615
